TPU v7x, 128 devices: a whole 4x4x4 slice. The times are simulated.
128 devices in a mesh: row: 16 (over y_lo, z, core), col: 8 (over y_hi, x).
Axes of the slice: x: 4, y: 4 (y_hi: 2, y_lo: 2; y = y_hi * 2 + y_lo), z: 4, core: 2. Of those that a mesh axis runs over, the one named last changes fastest.
Arguments:
- features: bfloat16 [98304, 256], P(('col', 'row')), may hold values from -6 to 6
- weight: bfloat16 [256, 256], replicated, may hold values from -0.375 to 0.375
- grad_out: bfloat16 [98304, 256], P(('row', 'col')), may hold values from -6 to 6
- tile_rows: int32 [16, 8, 608], P('row', 'col'), may hold values from 0 to 95
- tile_cols: int32 [16, 8, 608], P('row', 'col'), may hold values from 0 to 191
- tile_values: bfloat16 [16, 8, 608, 4096], P('row', 'col'), may hold values from 0 to 0.1, as said below
- tile_counts: int32 [16, 8], P('row', 'col'), may hold values from 76 to 608, as said below
Outputs:
- output: bfloat16 [98304, 256], P(('row', 'col'))
- grad_feat: bfloat16 [98304, 256], P(('col', 'row'))
- grad_weight: float32 [256, 256], replicated
Inputs may be any that keep to these rules, and one draw needn't show every extreme that they name: `tile_values`: tile values are zero or positive; about 3 percent of a tile's entries are nonzero, lying in about a quarter of its rows and a quarter of its columns. `tile_counts`: each count is 608, 304, 152 or 76, and some device holds 608.
All inputs are finite; a program needn't handle non-finite values.
Results may differ from a plain program's by a relative error of at most 0.022.
Values may be sent and summed in bfloat16 or wider, within the bound.
A program may use at most 192 MiB of HBM per device.

v0:
```python
import jax
import jax.numpy as jnp
from jax import lax
from jax.sharding import PartitionSpec as P

BLOCK = 64
GROUP = 152


def activate(z):
    return jax.nn.gelu(z, approximate=True)


def tile_apply(values, rows, cols, count, source, out_blocks, flip):
    tiles = values.shape[2]
    group = min(GROUP, tiles)
    blocks = values.reshape(tiles, BLOCK, BLOCK)
    width = source.shape[1]
    pieces = source.reshape(-1, BLOCK, width)
    rows_flat = rows.reshape(tiles)
    cols_flat = cols.reshape(tiles)
    take, put = (rows_flat, cols_flat) if flip else (cols_flat, rows_flat)
    live_total = count.reshape(())

    def step(index, total):
        start = index * group
        chosen = lax.dynamic_slice_in_dim(blocks, start, group, 0)
        take_now = lax.dynamic_slice_in_dim(take, start, group, 0)
        put_now = lax.dynamic_slice_in_dim(put, start, group, 0)
        live = start + jnp.arange(group, dtype=jnp.int32) < live_total
        chosen = jnp.where(live[:, None, None], chosen, jnp.zeros_like(chosen))
        picked = pieces[take_now]
        if flip:
            product = jnp.einsum("tji,tjd->tid", chosen, picked, preferred_element_type=jnp.float32)
        else:
            product = jnp.einsum("tij,tjd->tid", chosen, picked, preferred_element_type=jnp.float32)
        return total.at[put_now].add(product)

    steps_needed = tiles // group
    total = lax.fori_loop(0, steps_needed, step, jnp.zeros((out_blocks, BLOCK, width), jnp.float32))
    return total.reshape(out_blocks * BLOCK, width)


def per_device(features, weight, grad_out, tile_rows, tile_cols, tile_values, tile_counts):
    nodes_dev = features.shape[0]
    row_count = lax.axis_size("row")
    col_count = lax.axis_size("col")
    source = lax.all_gather(features, "row", axis=0, tiled=True)
    partial_value = tile_apply(
        tile_values,
        tile_rows,
        tile_cols,
        tile_counts,
        source,
        nodes_dev * col_count // BLOCK,
        False,
    )
    hidden = lax.psum_scatter(
        partial_value.astype(jnp.bfloat16), "col", scatter_dimension=0, tiled=True
    )
    pre = jnp.dot(hidden, weight, preferred_element_type=jnp.float32)
    output = activate(pre).astype(jnp.bfloat16)
    grad_pre = jax.vjp(activate, pre)[1](grad_out.astype(jnp.float32))[0].astype(jnp.bfloat16)
    term = jnp.einsum("nd,ne->de", hidden, grad_pre, preferred_element_type=jnp.float32)
    grad_weight = lax.psum(term, ("row", "col"))
    grad_local = jnp.einsum(
        "ne,de->nd", grad_pre, weight, preferred_element_type=jnp.float32
    ).astype(jnp.bfloat16)
    grad_hidden = lax.all_gather(grad_local, "col", axis=0, tiled=True)
    backward = tile_apply(
        tile_values,
        tile_rows,
        tile_cols,
        tile_counts,
        grad_hidden,
        nodes_dev * row_count // BLOCK,
        True,
    )
    grad_feat = lax.psum_scatter(
        backward.astype(jnp.bfloat16), "row", scatter_dimension=0, tiled=True
    )
    return (output, grad_feat, grad_weight)


def solution(mesh):
    placed = (
        P(("col", "row"), None),
        P(),
        P(("row", "col"), None),
        P("row", "col", None),
        P("row", "col", None),
        P("row", "col", None, None),
        P("row", "col"),
    )
    return jax.shard_map(
        per_device,
        mesh=mesh,
        in_specs=placed,
        out_specs=(P(("row", "col"), None), P(("col", "row"), None), P()),
        check_vma=False,
    )
```

profile of v0, /device:TPU:0, one launch (start us, length us, event | category | flops | bytes accessed | tf_op | source)
XLA Modules:
  0.0 782.6 jit_solution(17259728086362496295)
XLA Ops:
  9.4 7.8 copy.11
  17.2 37.5 %all-gather.3.cloned.1.call-done = bf16[12288,256]{1,0:T(8,128)(2,1)} async-done(((bf16[768,256]{1,0:T(8,128)(2,1)}), bf16[12288,256]{1,0:T(8,128)(2,1)}) %all-gather.3.cloned.1.call-update) | async-done | bytes 6291472 | tf_op jit(solution)/shard_map/all_gather | solution.py:48
  58.1 239.1 %while.26 = (s32[]{:T(128)}, f32[96,64,256]{2,1,0:T(8,128)}, s32[608]{0:T(1024)S(1)}, s32[]{:T(128)}, bf16[608,64,64]{0,2,1:T(8,128)(2,1)}, /*index=5*/s32[608]{...) while((s32[]{:T(128)}, f32[96,64,256]{2,1,0:T(8,128)}, ...), condition=%wide.region_2.3_spmd, body=%wide.region_0.2_spmd.sunk | while | flops 321882304 | bytes 61022840 | solution.py:40
  66.9 10.5 %gather_fusion = bf16[152,64,256]{2,1,0:T(8,128)(2,1)} fusion(bf16[192,64,256]{2,1,0:T(8,128)(2,1)} %get-tuple-element.430, s32[1024]{0:T(1024)S(1)} %pad_clamp_fusion.4), kind=kCustom, calls=%fused_computation.clone.1 | custom fusion | bytes 9962080 | tf_op jit(solution)/shard_map/while/body/eval_jaxpr/gather | solution.py:32
  77.4 7.7 fusion.37
  85.1 32.9 %scatter_fusion = f32[96,64,256]{2,1,0:T(8,128)} fusion(f32[96,64,256]{2,1,0:T(8,128)} %get-tuple-element.414, s32[152]{0:T(256)S(1)} %get-tuple-element.391, f32[152,64,256]{2,1,0:T(8,128)} %fusion.37), kind=kCustom, calls=%fused_computation.2.clone.1 | custom fusion | flops 2490368 | bytes 29885024 | tf_op jit(solution)/shard_map/while/body/eval_jaxpr/scatter-add | solution.py:37
  126.9 10.5 %gather_fusion = bf16[152,64,256]{2,1,0:T(8,128)(2,1)} fusion(bf16[192,64,256]{2,1,0:T(8,128)(2,1)} %get-tuple-element.430, s32[1024]{0:T(1024)S(1)} %pad_clamp_fusion.4), kind=kCustom, calls=%fused_computation.clone.1 | custom fusion | bytes 9962080 | tf_op jit(solution)/shard_map/while/body/eval_jaxpr/gather | solution.py:32
  137.3 7.7 fusion.37
  145.1 32.9 %scatter_fusion = f32[96,64,256]{2,1,0:T(8,128)} fusion(f32[96,64,256]{2,1,0:T(8,128)} %get-tuple-element.414, s32[152]{0:T(256)S(1)} %get-tuple-element.391, f32[152,64,256]{2,1,0:T(8,128)} %fusion.37), kind=kCustom, calls=%fused_computation.2.clone.1 | custom fusion | flops 2490368 | bytes 29885024 | tf_op jit(solution)/shard_map/while/body/eval_jaxpr/scatter-add | solution.py:37
  186.8 10.5 %gather_fusion = bf16[152,64,256]{2,1,0:T(8,128)(2,1)} fusion(bf16[192,64,256]{2,1,0:T(8,128)(2,1)} %get-tuple-element.430, s32[1024]{0:T(1024)S(1)} %pad_clamp_fusion.4), kind=kCustom, calls=%fused_computation.clone.1 | custom fusion | bytes 9962080 | tf_op jit(solution)/shard_map/while/body/eval_jaxpr/gather | solution.py:32
  197.3 7.7 fusion.37
  205.0 32.7 %scatter_fusion = f32[96,64,256]{2,1,0:T(8,128)} fusion(f32[96,64,256]{2,1,0:T(8,128)} %get-tuple-element.414, s32[152]{0:T(256)S(1)} %get-tuple-element.391, f32[152,64,256]{2,1,0:T(8,128)} %fusion.37), kind=kCustom, calls=%fused_computation.2.clone.1 | custom fusion | flops 2490368 | bytes 29885024 | tf_op jit(solution)/shard_map/while/body/eval_jaxpr/scatter-add | solution.py:37
  246.3 10.5 %gather_fusion = bf16[152,64,256]{2,1,0:T(8,128)(2,1)} fusion(bf16[192,64,256]{2,1,0:T(8,128)(2,1)} %get-tuple-element.430, s32[1024]{0:T(1024)S(1)} %pad_clamp_fusion.4), kind=kCustom, calls=%fused_computation.clone.1 | custom fusion | bytes 9962080 | tf_op jit(solution)/shard_map/while/body/eval_jaxpr/gather | solution.py:32
  256.8 7.7 fusion.37
  264.5 32.7 %scatter_fusion = f32[96,64,256]{2,1,0:T(8,128)} fusion(f32[96,64,256]{2,1,0:T(8,128)} %get-tuple-element.414, s32[152]{0:T(256)S(1)} %get-tuple-element.391, f32[152,64,256]{2,1,0:T(8,128)} %fusion.37), kind=kCustom, calls=%fused_computation.2.clone.1 | custom fusion | flops 2490368 | bytes 29885024 | tf_op jit(solution)/shard_map/while/body/eval_jaxpr/scatter-add | solution.py:37
  302.3 81.4 %reduce-scatter.3.cloned.1.call-done = bf16[768,256]{1,0:T(8,128)(2,1)} async-done(((bf16[6144,256]{1,0:T(8,128)(2,1)}), bf16[768,256]{1,0:T(8,128)(2,1)}) %reduce-scatter.3.cloned.1.call-update) | async-done | bytes 393232 | tf_op jit(solution)/shard_map/reduce_scatter | solution.py:58
  388.6 60.7 %all-gather.5.cloned.1.call-done = bf16[6144,256]{1,0:T(8,128)(2,1)} async-done(((bf16[768,256]{1,0:T(8,128)(2,1)}), bf16[6144,256]{1,0:T(8,128)(2,1)}) %all-gather.5.cloned.1.call-update) | async-done | bytes 3145744 | tf_op jit(solution)/shard_map/all_gather | solution.py:69
  455.4 241.2 %while.27 = (s32[]{:T(128)}, f32[192,64,256]{2,1,0:T(8,128)}, s32[608]{0:T(1024)S(1)}, s32[]{:T(128)}, bf16[608,64,64]{0,2,1:T(8,128)(2,1)}, /*index=5*/s32[608]...) while((s32[]{:T(128)}, f32[192,64,256]{2,1,0:T(8,128)}, ...), condition=%wide.region_6.0_spmd, body=%wide.region_4.0_spmd.sunk | while | flops 321882304 | bytes 61022840 | solution.py:40
  465.7 9.6 %gather_fusion.1 = bf16[152,64,256]{2,1,0:T(8,128)(2,1)} fusion(bf16[96,64,256]{2,1,0:T(8,128)(2,1)} %get-tuple-element.463, s32[1024]{0:T(1024)S(1)} %pad_clamp_fusion.5), kind=kCustom, calls=%fused_computation.1.clone.1 | custom fusion | bytes 9962080 | tf_op jit(solution)/shard_map/while/body/eval_jaxpr/gather | solution.py:32
  475.3 7.7 fusion.40
  482.9 32.9 %scatter_fusion.1 = f32[192,64,256]{2,1,0:T(8,128)} fusion(f32[192,64,256]{2,1,0:T(8,128)} %get-tuple-element.447, s32[152]{0:T(256)S(1)} %get-tuple-element.400, f32[152,64,256]{2,1,0:T(8,128)} %fusion.40), kind=kCustom, calls=%fused_computation.3.clone.1 | custom fusion | flops 2490368 | bytes 29885024 | tf_op jit(solution)/shard_map/while/body/eval_jaxpr/scatter-add | solution.py:37
  526.1 9.6 %gather_fusion.1 = bf16[152,64,256]{2,1,0:T(8,128)(2,1)} fusion(bf16[96,64,256]{2,1,0:T(8,128)(2,1)} %get-tuple-element.463, s32[1024]{0:T(1024)S(1)} %pad_clamp_fusion.5), kind=kCustom, calls=%fused_computation.1.clone.1 | custom fusion | bytes 9962080 | tf_op jit(solution)/shard_map/while/body/eval_jaxpr/gather | solution.py:32
  535.7 7.7 fusion.40
  543.4 33.0 %scatter_fusion.1 = f32[192,64,256]{2,1,0:T(8,128)} fusion(f32[192,64,256]{2,1,0:T(8,128)} %get-tuple-element.447, s32[152]{0:T(256)S(1)} %get-tuple-element.400, f32[152,64,256]{2,1,0:T(8,128)} %fusion.40), kind=kCustom, calls=%fused_computation.3.clone.1 | custom fusion | flops 2490368 | bytes 29885024 | tf_op jit(solution)/shard_map/while/body/eval_jaxpr/scatter-add | solution.py:37
  586.6 9.6 %gather_fusion.1 = bf16[152,64,256]{2,1,0:T(8,128)(2,1)} fusion(bf16[96,64,256]{2,1,0:T(8,128)(2,1)} %get-tuple-element.463, s32[1024]{0:T(1024)S(1)} %pad_clamp_fusion.5), kind=kCustom, calls=%fused_computation.1.clone.1 | custom fusion | bytes 9962080 | tf_op jit(solution)/shard_map/while/body/eval_jaxpr/gather | solution.py:32
  596.2 7.7 fusion.40
  603.8 32.8 %scatter_fusion.1 = f32[192,64,256]{2,1,0:T(8,128)} fusion(f32[192,64,256]{2,1,0:T(8,128)} %get-tuple-element.447, s32[152]{0:T(256)S(1)} %get-tuple-element.400, f32[152,64,256]{2,1,0:T(8,128)} %fusion.40), kind=kCustom, calls=%fused_computation.3.clone.1 | custom fusion | flops 2490368 | bytes 29885024 | tf_op jit(solution)/shard_map/while/body/eval_jaxpr/scatter-add | solution.py:37
  646.6 9.6 %gather_fusion.1 = bf16[152,64,256]{2,1,0:T(8,128)(2,1)} fusion(bf16[96,64,256]{2,1,0:T(8,128)(2,1)} %get-tuple-element.463, s32[1024]{0:T(1024)S(1)} %pad_clamp_fusion.5), kind=kCustom, calls=%fused_computation.1.clone.1 | custom fusion | bytes 9962080 | tf_op jit(solution)/shard_map/while/body/eval_jaxpr/gather | solution.py:32
  656.2 7.7 fusion.40
  663.8 32.8 %scatter_fusion.1 = f32[192,64,256]{2,1,0:T(8,128)} fusion(f32[192,64,256]{2,1,0:T(8,128)} %get-tuple-element.447, s32[152]{0:T(256)S(1)} %get-tuple-element.400, f32[152,64,256]{2,1,0:T(8,128)} %fusion.40), kind=kCustom, calls=%fused_computation.3.clone.1 | custom fusion | flops 2490368 | bytes 29885024 | tf_op jit(solution)/shard_map/while/body/eval_jaxpr/scatter-add | solution.py:37
  696.7 8.2 %convert_element_type.30 = bf16[192,64,256]{2,1,0:T(8,128)(2,1)} convert(f32[192,64,256]{2,1,0:T(8,128)} %get-tuple-element.252) | non-fusion elementwise | flops 3145728 | bytes 18874368 | tf_op jit(solution)/shard_map/convert_element_type | solution.py:80
  704.9 69.5 %reduce-scatter.5.cloned.1.call-done = bf16[768,256]{1,0:T(8,128)(2,1)} async-done(((bf16[12288,256]{1,0:T(8,128)(2,1)}), bf16[768,256]{1,0:T(8,128)(2,1)}) %reduce-scatter.5.cloned.1.call-update) | async-done | bytes 393232 | tf_op jit(solution)/shard_map/reduce_scatter | solution.py:79
  (68 shorter events, 99.1 us)
Async XLA Ops:
  7.2 376.5 %copy-start = (bf16[256,256]{1,0:T(8,128)(2,1)S(1)}, bf16[256,256]{1,0:T(8,128)(2,1)}, u32[]{:S(2)}) copy-start(bf16[256,256]{1,0:T(8,128)(2,1)} %param.12) | copy-start | bytes 393220
  7.2 47.5 %all-gather.3.cloned.1.call-start = ((), (), s32[]{:S(2)}) async-start(), calls=%async_computation.2 | async-start | bytes 6684672 | tf_op jit(solution)/shard_map/all_gather | solution.py:48
  7.9 375.7 %reduce-scatter.3.cloned.1.call-start = ((), (), s32[]{:S(2)}) async-start(), calls=%async_computation.3 | async-start | bytes 3538944 | tf_op jit(solution)/shard_map/reduce_scatter | solution.py:58
  297.2 86.4 %copy-start.3 = (bf16[768,256]{1,0:T(8,128)(2,1)S(1)}, bf16[768,256]{1,0:T(8,128)(2,1)}, u32[]{:S(2)}) copy-start(bf16[768,256]{1,0:T(8,128)(2,1)} %param.13) | copy-start | bytes 1179652
  302.2 147.1 %all-gather.5.cloned.1.call-start = ((), (), s32[]{:S(2)}) async-start(), calls=%async_computation.4 | async-start | bytes 3538944 | tf_op jit(solution)/shard_map/all_gather | solution.py:69
  383.6 3.7 copy-start.2
  387.3 317.6 %all-reduce.2.cloned.1.call-start = ((), (), s32[]{:S(2)}) async-start(), calls=%async_computation.6 | async-start | bytes 524288 | tf_op jit(solution)/shard_map/psum | solution.py:65
  388.4 386.1 %reduce-scatter.5.cloned.1.call-start = ((), (), s32[]{:S(2)}) async-start(), calls=%async_computation.5 | async-start | bytes 6684672 | tf_op jit(solution)/shard_map/reduce_scatter | solution.py:79
  696.7 79.5 %copy-start.1 = (bf16[256,256]{1,0:T(8,128)(2,1)S(1)}, bf16[256,256]{1,0:T(8,128)(2,1)}, u32[]{:S(2)}) copy-start(bf16[256,256]{1,0:T(8,128)(2,1)} %param.12) | copy-start | bytes 393220
Sparse Core Ops, SparseCore 0:
  9.7 44.8 all-gather.2
  302.3 81.2 reduce-scatter.2
  387.4 61.8 all-gather.4
  455.2 140.3 all-reduce.1
  705.0 69.4 reduce-scatter.4
where the time goes:
time: 787 us; the launch traced here: 783 us
  other arithmetic  283 us (36%)
  waiting for transfers between devices  250 us (32%)
  local copies, waits for them, and re-layouts  169 us (21%)
  matrix products  66.2 us (8%)
  between operations  13.8 us (2%)
    scatter-add x8, other arithmetic, step(): return total.at[put_now].add(product)  263 us
    reduce_scatter x1, waiting for transfers between devices, per_device(): lax.psum_scatter(partial_value.astype(jnp.bfloat16), 'col', scatter_dimen...  81.4 us
    gather x8, local copies, waits for them, and re-layouts, step(): picked = pieces[take_now]  80.1 us
    dynamic_slice x16, local copies, waits for them, and re-layouts, step(): chosen = lax.dynamic_slice_in_dim(blocks, start, group, 0)  69.8 us
    reduce_scatter x1, waiting for transfers between devices, per_device(): lax.psum_scatter(backward.astype(jnp.bfloat16), 'row', scatter_dimension=...  69.5 us
    all_gather x1, waiting for transfers between devices, per_device(): grad_hidden = lax.all_gather(grad_local, 'col', axis=0, tiled=True)  60.7 us
    all_gather x1, waiting for transfers between devices, per_device(): source = lax.all_gather(features, 'row', axis=0, tiled=True)  37.5 us
    dot_general x4, matrix products, step(): jnp.einsum('tij,tjd->tid', chosen, picked, preferred_element_type=jnp.flo...  30.9 us
  transfers between devices with their start and end apart: 5, of which 4 were waited for; matrix products, arithmetic and copies ran while one was open for 34% of the time, Pallas kernels for 0%

commit v1 on v0

v1 whole, which is shorter than its diff:
```python
import functools
import jax, jax.numpy as jnp
from jax import lax
from jax.experimental import pallas as pl
from jax.experimental.pallas import tpu as pltpu
from jax.sharding import PartitionSpec as P

BLOCK = 64
GROUP = 4
f32, bf16, i32 = jnp.float32, jnp.bfloat16, jnp.int32


def meta_one(key_row, other_row, tiles, nb, slots):
    tp = key_row.shape[1]
    nbp = -(-nb // 128) * 128
    hot = lax.broadcasted_iota(i32, (nbp, tp), 0) == key_row
    hotf = hot.astype(f32)
    hotb = hotf.astype(bf16)
    count = jnp.sum(hotf, axis=1, keepdims=True)
    upper = (lax.broadcasted_iota(i32, (tp, tp), 0) < lax.broadcasted_iota(i32, (tp, tp), 1)).astype(f32).astype(bf16)
    rank = jnp.dot(hotb, upper, preferred_element_type=f32)
    groups = jnp.floor((count + (GROUP - 1)) * (1.0 / GROUP))
    lower = (lax.broadcasted_iota(i32, (nbp, nbp), 1) < lax.broadcasted_iota(i32, (nbp, nbp), 0)).astype(f32).astype(bf16)
    first = jnp.dot(lower, jnp.broadcast_to(groups, (nbp, 128)).astype(bf16), preferred_element_type=f32)[:, :1]
    place = jnp.sum(hotf * (rank + GROUP * first), axis=0, keepdims=True)
    live = jnp.sum(hotf, axis=0, keepdims=True) > 0
    place = jnp.where(live, place, -1.0).astype(i32)
    spot = (lax.broadcasted_iota(i32, (slots, tp), 0) == place).astype(f32).astype(bf16)
    t = lax.broadcasted_iota(i32, (1, tp), 1)
    row = lax.broadcasted_iota(i32, (8, tp), 0)
    data = jnp.where(row == 0, t // 128, jnp.where(row == 1, t % 128, jnp.where(row == 2, other_row, 1)))
    data = data.astype(f32).astype(bf16)
    got = lax.dot_general(data, spot, (((1,), (1,)), ((), ())), preferred_element_type=f32)
    there = got[3:4] > 0
    tile = jnp.where(there, got[0:1] * 128 + got[1:2], float(tiles)).astype(i32)
    other = jnp.where(there, got[2:3], 0.0).astype(i32)
    glanes = -(-(slots // GROUP) // 128) * 128
    ends = first + groups
    gi = lax.broadcasted_iota(i32, (nbp, glanes), 1).astype(f32)
    real = lax.broadcasted_iota(i32, (nbp, glanes), 0) < nb
    owner = jnp.sum(jnp.where(jnp.logical_and(ends <= gi, real), 1.0, 0.0), axis=0, keepdims=True).astype(i32)
    total = jnp.sum(groups, axis=0, keepdims=True).astype(i32)
    return tile, other, owner, total


def meta_kernel(tiles, nr, nc, slots_f, slots_b, rows_ref, cols_ref, count_ref,
                ft, fo, fb, bt, bo, bb, tot):
    tp = rows_ref.shape[1]
    live = lax.broadcasted_iota(i32, (1, tp), 1) < count_ref[0, 0]
    rows = rows_ref[...]
    cols = cols_ref[...]
    a, b, c, d = meta_one(jnp.where(live, rows, 4096), cols, tiles, nr, slots_f)
    ft[...], fo[...], fb[...] = a, b, c
    e, f, g, h = meta_one(jnp.where(live, cols, 4096), rows, tiles, nc, slots_b)
    bt[...], bo[...], bb[...] = e, f, g
    lane = lax.broadcasted_iota(i32, (1, 128), 1)
    tot[...] = jnp.where(lane == 0, d, h)


def up(n, m):
    return -(-n // m) * m


def make_meta(rows, cols, count, nr, nc):
    tiles = rows.shape[-1]
    tp = up(tiles, 128)
    pad = lambda v: jnp.pad(v.reshape(1, tiles), ((0, 0), (0, tp - tiles)))
    slots_f = up(tiles + 3 * min(nr, tiles), 512)
    slots_b = up(tiles + 3 * min(nc, tiles), 512)
    shapes = []
    for s in (slots_f, slots_b):
        shapes += [jax.ShapeDtypeStruct((1, s), i32)] * 2 + [jax.ShapeDtypeStruct((1, up(s // GROUP, 128)), i32)]
    shapes.append(jax.ShapeDtypeStruct((1, 128), i32))
    return pl.pallas_call(
        functools.partial(meta_kernel, tiles, nr, nc, slots_f, slots_b),
        out_shape=shapes,
        in_specs=[pl.BlockSpec(memory_space=pltpu.VMEM)] * 2 + [pl.BlockSpec(memory_space=pltpu.SMEM)],
        out_specs=[pl.BlockSpec(memory_space=pltpu.VMEM)] * 7,
        compiler_params=pltpu.CompilerParams(vmem_limit_bytes=48 << 20),
        name="meta",
    )(pad(rows), pad(cols), count.reshape(1, 1))


def swap_halves(m):
    return jnp.concatenate([m[:, 64:], m[:, :64]], axis=1)


def fwd_kernel(tiles, unroll, tot_ref, t_ref, o_ref, b_ref, m_ref, src_ref, out_ref, acc):
    low = lax.broadcasted_iota(i32, (32, 128), 1) < 64
    acc[...] = jnp.zeros_like(acc)

    def lhs_of(g):
        m = [m_ref[t_ref[0, g * 4 + k]] for k in range(4)]
        s = [swap_halves(v) for v in m]
        ev = [jnp.where(low, m[0], s[1]), jnp.where(low, m[2], s[3])]
        od = [jnp.where(low, s[0], m[1]), jnp.where(low, s[2], m[3])]
        return jnp.concatenate([jnp.concatenate(ev, axis=1), jnp.concatenate(od, axis=1)], axis=0)

    def body(i, _):
        prods = []
        for u in range(unroll):
            g = i * unroll + u
            rhs = jnp.concatenate([src_ref[o_ref[0, g * 4 + k]] for k in range(4)], axis=0)
            prods.append((b_ref[0, g], jnp.dot(lhs_of(g), rhs, preferred_element_type=f32)))
        for b, p in prods:
            acc[b] += p
        return 0

    lax.fori_loop(0, (tot_ref[0, 0] + unroll - 1) // unroll, body, 0)
    for s in range(out_ref.shape[0] // 8):
        out_ref[s * 8:s * 8 + 8] = acc[s * 8:s * 8 + 8].astype(bf16)


def bwd_kernel(tiles, unroll, tot_ref, t_ref, o_ref, b_ref, m_ref, src_ref, out_ref, acc):
    acc[...] = jnp.zeros_like(acc)

    def body(i, _):
        prods = []
        for u in range(unroll):
            g = i * unroll + u
            w = jnp.concatenate([m_ref[t_ref[0, g * 4 + k]] for k in range(4)], axis=0).T
            lhs = jnp.concatenate([w[:64], w[64:]], axis=1)
            src = [src_ref[o_ref[0, g * 4 + k]] for k in range(4)]
            rhs = jnp.concatenate([v[:32] for v in src] + [v[32:] for v in src], axis=0)
            prods.append((b_ref[0, g], jnp.dot(lhs, rhs, preferred_element_type=f32)))
        for b, p in prods:
            acc[b] += p
        return 0

    lax.fori_loop(0, (tot_ref[0, 1] + unroll - 1) // unroll, body, 0)
    for s in range(out_ref.shape[0] // 8):
        out_ref[s * 8:s * 8 + 8] = acc[s * 8:s * 8 + 8].astype(bf16)


def spmm(kernel, meta3, tot, m, src, nb, name, unroll=2):
    tiles = m.shape[0]
    width = src.shape[1]
    return pl.pallas_call(
        functools.partial(kernel, tiles, unroll),
        out_shape=jax.ShapeDtypeStruct((nb, BLOCK, width), bf16),
        in_specs=[pl.BlockSpec(memory_space=pltpu.SMEM)] * 4 + [pl.BlockSpec(memory_space=pltpu.VMEM)] * 2,
        out_specs=pl.BlockSpec(memory_space=pltpu.VMEM),
        scratch_shapes=[pltpu.VMEM((nb + 1, BLOCK, width), f32)],
        compiler_params=pltpu.CompilerParams(vmem_limit_bytes=56 << 20),
        name=name,
    )(tot, *meta3, m, src.reshape(-1, BLOCK, width))


def relayout(values):
    tiles = values.shape[2]
    m = values.reshape(tiles, 32, 128)
    return jnp.concatenate([m, jnp.zeros((1, 32, 128), bf16)], axis=0)


def activate(z):
    return jax.nn.gelu(z, approximate=True)


def per_device(features, weight, grad_out, tile_rows, tile_cols, tile_values, tile_counts):
    nodes_dev, width = features.shape
    nr = nodes_dev * lax.axis_size("col") // BLOCK
    nc = nodes_dev * lax.axis_size("row") // BLOCK
    source = lax.all_gather(features, "row", axis=0, tiled=True)
    *lists, tot = make_meta(tile_rows, tile_cols, tile_counts, nr, nc)
    m = relayout(tile_values)
    part = spmm(fwd_kernel, lists[:3], tot, m, source, nr, "spmm_fwd")
    hidden = lax.psum_scatter(part.reshape(-1, width), "col", scatter_dimension=0, tiled=True)
    hidden = hidden.reshape(-1, 2, BLOCK // 2, width).swapaxes(1, 2).reshape(nodes_dev, width)
    pre = jnp.dot(hidden, weight, preferred_element_type=f32)
    output = activate(pre).astype(bf16)
    grad_pre = jax.vjp(activate, pre)[1](grad_out.astype(f32))[0].astype(bf16)
    term = jnp.einsum("nd,ne->de", hidden, grad_pre, preferred_element_type=f32)
    grad_weight = lax.psum(term, ("row", "col"))
    grad_local = jnp.einsum("ne,de->nd", grad_pre, weight, preferred_element_type=f32).astype(bf16)
    grad_local = grad_local.reshape(-1, BLOCK // 2, 2, width).swapaxes(1, 2).reshape(nodes_dev, width)
    grad_hidden = lax.all_gather(grad_local, "col", axis=0, tiled=True)
    back = spmm(bwd_kernel, lists[3:], tot, m, grad_hidden, nc, "spmm_bwd")
    grad_feat = lax.psum_scatter(back.reshape(-1, width), "row", scatter_dimension=0, tiled=True)
    return output, grad_feat, grad_weight


def solution(mesh):
    placed = (
        P(("col", "row"), None),
        P(),
        P(("row", "col"), None),
        P("row", "col", None),
        P("row", "col", None),
        P("row", "col", None, None),
        P("row", "col"),
    )
    return jax.shard_map(
        per_device,
        mesh=mesh,
        in_specs=placed,
        out_specs=(P(("row", "col"), None), P(("col", "row"), None), P()),
        check_vma=False,
    )
```

time: 787 us -> 455 us (0.58)
  other arithmetic: 283 us -> 0 us
  local copies, waits for them, and re-layouts: 169 us -> 16.8 us
  waiting for transfers between devices: 250 us -> 375 us
  matrix products: 66.2 us -> 2.81 us
  Pallas kernels: 0 us -> 45.1 us
    scatter-add x8 -> x0, other arithmetic: 263 us -> none  [step(): return total.at[put_now].add(product)]
    psum x1, waiting for transfers between devices: 0.02 us -> 123 us  [per_device(): grad_weight = lax.psum(term, ('row', 'col'))]
    gather x8 -> x0, local copies, waits for them, and re-layouts: 80.1 us -> none  [step(): picked = pieces[take_now]]
    dynamic_slice x16 -> x0, local copies, waits for them, and re-layouts: 69.8 us -> none  [step(): chosen = lax.dynamic_slice_in_dim(blocks, start, group, 0)]
    dot_general x11 -> x3, matrix products: 66.2 us -> 2.81 us  [the longest x1 1.51 us: per_device(): pre = jnp.dot(hidden, weight, preferred_element_type=f32)]
    pallas_call x0 -> x3, Pallas kernels: none -> 45.1 us  [the longest x2 43.3 us: spmm(): pl.pallas_call(functools.partial(kernel, tiles, unroll), out_shape=jax.Sh...]
    convert_element_type x2 -> x0, other arithmetic: 13.1 us -> none  [the longest x1 8.18 us: per_device(): backward.astype(jnp.bfloat16)]
    broadcast_in_dim x2 -> x0, local copies, waits for them, and re-layouts: 9.58 us -> none  [tile_apply(): jnp.zeros((out_blocks, BLOCK, width), jnp.float32)]
  transfers between devices with their start and end apart: 5 -> 5, of which waited for: 4 -> 5; matrix products, arithmetic and copies ran while one was open for 34% -> 2% of each run, Pallas kernels for 0% -> 6%
where the time goes in v1:
time: 455 us; the launch traced here: 454 us
  waiting for transfers between devices  375 us (82%)
  Pallas kernels  45.1 us (10%)
  local copies, waits for them, and re-layouts  16.8 us (4%)
  between operations  14.5 us (3%)
    psum x1, waiting for transfers between devices, per_device(): grad_weight = lax.psum(term, ('row', 'col'))  123 us
    reduce_scatter x1, waiting for transfers between devices, per_device(): lax.psum_scatter(part.reshape(-1, width), 'col', scatter_dimension=0, til...  88.2 us
    reduce_scatter x1, waiting for transfers between devices, per_device(): lax.psum_scatter(back.reshape(-1, width), 'row', scatter_dimension=0, til...  71 us
    all_gather x1, waiting for transfers between devices, per_device(): grad_hidden = lax.all_gather(grad_local, 'col', axis=0, tiled=True)  60.9 us
    pallas_call x2, Pallas kernels, spmm(): pl.pallas_call(functools.partial(kernel, tiles, unroll), out_shape=jax.Sh...  43.3 us
    all_gather x1, waiting for transfers between devices, per_device(): source = lax.all_gather(features, 'row', axis=0, tiled=True)  31.7 us
    unnamed x20, local copies, waits for them, and re-layouts  9.67 us
  transfers between devices with their start and end apart: 5, of which 5 were waited for; matrix products, arithmetic and copies ran while one was open for 2% of the time, Pallas kernels for 6%

profile of v1, /device:TPU:0, one launch (start us, length us, event | category | flops | bytes accessed | tf_op | source)
XLA Modules:
  0.0 454.4 jit_solution(8301961904415777235)
XLA Ops:
  7.2 0.7 all-gather.3.cloned.1.call-update
  7.9 0.0 reduce-scatter.3.cloned.1.call-start
  8.0 0.7 pad.8.rows_ref
  8.7 0.7 pad.9.cols_ref
  10.0 3.9 copy.14
  13.9 3.2 concatenate.3.m_ref
  17.1 1.8 meta.1
  18.9 0.6 copy-done.1
  19.5 0.6 copy-done.2
  20.1 0.6 copy-done.3
  20.7 0.6 copy-done.4
  21.3 0.5 copy-done.5
  21.8 0.6 copy-done.6
  22.4 0.6 copy-done.7
  23.0 31.7 %all-gather.3.cloned.1.call-done = bf16[12288,256]{1,0:T(8,128)(2,1)} async-done(((bf16[768,256]{1,0:T(8,128)(2,1)}), bf16[12288,256]{1,0:T(8,128)(2,1)}) %all-gather.3.cloned.1.call-update) | async-done | bytes 6291472 | tf_op jit(solution)/shard_map/all_gather | solution.py:163
  54.7 19.4 %spmm_fwd.1 = bf16[96,64,256]{2,1,0:T(8,128)(2,1)} custom-call(s32[1,128]{1,0:T(1,128)} %copy-done.5, s32[1,1024]{1,0:T(1,128)} %copy-done.3, s32[1,1024]{1,0:T(1,128)} %copy-done.4, s32[1,256]{1,0:T(1,128)} %copy-done.7, bf16[609,32,128]{2,1,0:T(8,128)(2,1)} %concatenate.3.m_ref, bf16[192,64,256]{2,1,0:T(8,128)(2,1)} %bitcast.24), custom_call_target="tpu_custom_call" | custom-call | tf_op jit(solution)/shard_map/spmm_fwd/pallas_call | solution.py:138
  74.0 0.0 all-gather.5.cloned.1.call-start
  74.1 88.2 %reduce-scatter.3.cloned.1.call-done = bf16[768,256]{1,0:T(8,128)(2,1)} async-done(((bf16[6144,256]{1,0:T(8,128)(2,1)}), bf16[768,256]{1,0:T(8,128)(2,1)}) %reduce-scatter.3.cloned.1.call-update) | async-done | bytes 393232 | tf_op jit(solution)/shard_map/reduce_scatter | solution.py:167
  162.3 1.4 copy.12
  163.7 0.2 reshape.45
  163.9 1.5 fusion.2
  165.4 0.3 convolution_convert_fusion
  165.7 0.2 reshape.46
  165.8 0.8 copy.13
  166.7 0.0 all-reduce.5.cloned.1.call-start
  166.7 1.0 fusion.10
  167.8 0.0 reduce-scatter.5.cloned.1.call-start
  167.8 60.9 %all-gather.5.cloned.1.call-done = bf16[6144,256]{1,0:T(8,128)(2,1)} async-done(((bf16[768,256]{1,0:T(8,128)(2,1)}), bf16[6144,256]{1,0:T(8,128)(2,1)}) %all-gather.5.cloned.1.call-update) | async-done | bytes 3145744 | tf_op jit(solution)/shard_map/all_gather | solution.py:176
  228.7 23.9 %spmm_bwd.1 = bf16[192,64,256]{2,1,0:T(8,128)(2,1)} custom-call(s32[1,128]{1,0:T(1,128)} %copy-done.5, s32[1,1536]{1,0:T(1,128)} %copy-done.1, s32[1,1536]{1,0:T(1,128)} %copy-done.2, s32[1,384]{1,0:T(1,128)} %copy-done.6, bf16[609,32,128]{2,1,0:T(8,128)(2,1)} %concatenate.3.m_ref, bf16[96,64,256]{2,1,0:T(8,128)(2,1)} %bitcast.26), custom_call_target="tpu_custom_call" | custom-call | tf_op jit(solution)/shard_map/spmm_bwd/pallas_call | solution.py:138
  252.6 122.6 %all-reduce.5.cloned.1.call-done = f32[256,256]{1,0:T(8,128)} async-done(((f32[256,256]{1,0:T(8,128)}), f32[256,256]{1,0:T(8,128)}) %all-reduce.5.cloned.1.call-update) | async-done | bytes 262160 | tf_op jit(solution)/shard_map/psum | solution.py:173
  375.2 71.0 %reduce-scatter.5.cloned.1.call-done = bf16[768,256]{1,0:T(8,128)(2,1)} async-done(((bf16[12288,256]{1,0:T(8,128)(2,1)}), bf16[768,256]{1,0:T(8,128)(2,1)}) %reduce-scatter.5.cloned.1.call-update) | async-done | bytes 393232 | tf_op jit(solution)/shard_map/reduce_scatter | solution.py:178
  446.2 1.7 copy.17
  (16 shorter events, 0.1 us)
Async XLA Ops:
  7.2 156.7 %copy-start = (bf16[256,256]{1,0:T(8,128)(2,1)S(1)}, bf16[256,256]{1,0:T(8,128)(2,1)}, u32[]{:S(2)}) copy-start(bf16[256,256]{1,0:T(8,128)(2,1)} %param.8) | copy-start | bytes 393220
  7.2 47.5 %all-gather.3.cloned.1.call-start = ((), (), s32[]{:S(2)}) async-start(), calls=%async_computation.2 | async-start | bytes 6684672 | tf_op jit(solution)/shard_map/all_gather | solution.py:163
  7.9 154.4 %reduce-scatter.3.cloned.1.call-start = ((), (), s32[]{:S(2)}) async-start(), calls=%async_computation.3 | async-start | bytes 3538944 | tf_op jit(solution)/shard_map/reduce_scatter | solution.py:167
  18.9 0.6 copy-start.1
  19.5 0.6 copy-start.2
  20.1 0.6 copy-start.3
  20.7 0.6 copy-start.4
  21.3 0.5 copy-start.5
  21.8 0.6 copy-start.6
  22.4 0.6 copy-start.7
  54.6 109.2 %copy-start.8 = (bf16[768,256]{1,0:T(8,128)(2,1)S(1)}, bf16[768,256]{1,0:T(8,128)(2,1)}, u32[]{:S(2)}) copy-start(bf16[768,256]{1,0:T(8,128)(2,1)} %param.9) | copy-start | bytes 1179652
  74.0 154.7 %all-gather.5.cloned.1.call-start = ((), (), s32[]{:S(2)}) async-start(), calls=%async_computation.4 | async-start | bytes 3538944 | tf_op jit(solution)/shard_map/all_gather | solution.py:176
  166.7 208.6 %all-reduce.5.cloned.1.call-start = ((), (), s32[]{:S(2)}) async-start(), calls=%async_computation.6 | async-start | bytes 524288 | tf_op jit(solution)/shard_map/psum | solution.py:173
  167.8 278.4 %reduce-scatter.5.cloned.1.call-start = ((), (), s32[]{:S(2)}) async-start(), calls=%async_computation.5 | async-start | bytes 6684672 | tf_op jit(solution)/shard_map/reduce_scatter | solution.py:178
Sparse Core Ops, SparseCore 0:
  9.7 44.8 all-gather.2
  74.2 88.0 reduce-scatter.2
  166.8 61.8 all-gather.4
  234.6 140.6 all-reduce.4
  378.2 67.9 reduce-scatter.4

commit v2 on v1

--- a/solution.py
+++ b/solution.py
@@ -151,31 +151,425 @@
     m = values.reshape(tiles, 32, 128)
     return jnp.concatenate([m, jnp.zeros((1, 32, 128), bf16)], axis=0)
 
-
-def activate(z):
-    return jax.nn.gelu(z, approximate=True)
+MESH = pl.DeviceIdType.MESH
+RING = 4
+ANY = pl.ANY
+VM = pltpu.VMEM
+
+
+class Wire:
+    def __init__(self, send_sem, recv_sem):
+        self.send_sem, self.recv_sem = send_sem, recv_sem
+        self.ids, self.sent = {}, []
+
+    def _sems(self, key):
+        n = self.ids.setdefault(key, len(self.ids))
+        assert n < self.send_sem.shape[0]
+        return dict(send_sem=self.send_sem.at[n], recv_sem=self.recv_sem.at[n])
+
+    def push(self, key, src, dst, dev):
+        copy = pltpu.make_async_remote_copy(
+            src_ref=src, dst_ref=dst, device_id=dev, device_id_type=MESH, **self._sems(key))
+        copy.start()
+        self.sent.append(copy)
+
+    def take(self, key, dst, dev):
+        pltpu.make_async_remote_copy(
+            src_ref=dst, dst_ref=dst, device_id=dev, device_id_type=MESH, **self._sems(key)).wait_recv()
+
+    def drain(self):
+        for copy in self.sent:
+            copy.wait_send()
+
+
+def barrier(devs):
+    sem = pltpu.get_barrier_semaphore()
+    for dev in devs:
+        pl.semaphore_signal(sem, inc=1, device_id=dev, device_id_type=MESH)
+    pl.semaphore_wait(sem, len(devs))
+
+
+def row_place():
+    r = lax.axis_index("row")
+    pair, ring, core = r // (2 * RING), (r // 2) % RING, r % 2
+
+    def blk(p, d, s=0):
+        return (pair + p) % 2 * (2 * RING) + (ring + d) % RING * 2 + (core + s) % 2
+
+    return blk, (lambda p, d, s=0: {"row": blk(p, d, s)}), core
+
+
+def col_place():
+    c = lax.axis_index("col")
+    pair, ring = c // RING, c % RING
+
+    def blk(p, d):
+        return (pair + p) % 2 * RING + (ring + d) % RING
+
+    return blk, (lambda p, d: {"col": blk(p, d)})
+
+
+def gather_kernel(nchunk, first_a, feat, out, send_sem, recv_sem, own_sem):
+    blk, dev, _ = row_place()
+    wire = Wire(send_sem, recv_sem)
+    rows = feat.shape[0] // nchunk
+    kind_a = [k for k in range(nchunk) if k < first_a]
+    kind_b = [k for k in range(nchunk) if k >= first_a]
+    to = {"R": dev(0, 1), "L": dev(0, -1), "Y": dev(1, 0), "S": dev(0, 0, 1)}
+    barrier(list(to.values()))
+    own = pltpu.make_async_copy(feat, out.at[blk(0, 0)], own_sem)
+    own.start()
+
+    def slot(p, d, s, k):
+        return out.at[blk(p, d, s), pl.ds(k * rows, rows)]
+
+    def push(way, p, d, k):
+        src = feat.at[pl.ds(k * rows, rows)] if (p, d) == (0, 0) else slot(p, d, 0, k)
+        wire.push((way, p, d, k), src, slot(p, d, 0, k), to[way])
+
+    def take(way, p, d, k):
+        if way == "S":
+            wire.take((way, p, d, k), slot(p, d, 1, k), to["S"])
+            return
+        q, e = {"R": (p, d - 1), "L": (p, d + 1), "Y": (1 - p, d)}[way]
+        wire.take((way, p, d, k), slot(q, e, 0, k), to["S"])
+        a = k in kind_a
+        if way == "Y":
+            if not a:
+                push("R", q, e, k)
+                push("L", q, e, k)
+        else:
+            if a:
+                push("Y", q, e, k)
+            if abs(e) == 1 and (k % 2 == 0) == (way == "R"):
+                push(way, q, e, k)
+        push("S", q, e, k)
+
+    for k in kind_b + kind_a:
+        push("Y", 0, 0, k)
+        push("R", 0, 0, k)
+        push("L", 0, 0, k)
+    for k in kind_b + kind_a:
+        push("S", 0, 0, k)
+    for k in kind_b:
+        take("Y", 0, 0, k)
+    for k in kind_a:
+        take("R", 0, 0, k)
+        take("L", 0, 0, k)
+    for k in kind_a:
+        take("Y", 0, 0, k)
+    for k in kind_b:
+        take("R", 0, 0, k)
+        take("L", 0, 0, k)
+    for k in kind_a:
+        take(*(("R", 0, -1, k) if k % 2 == 0 else ("L", 0, 1, k)))
+    for k in kind_b:
+        take("R", 1, 0, k)
+        take("L", 1, 0, k)
+    for k in kind_a:
+        take("Y", 0, -1, k)
+        take("Y", 0, 1, k)
+    for p in (0, 1):
+        for k in kind_b:
+            take(*(("R", p, -1, k) if k % 2 == 0 else ("L", p, 1, k)))
+    for k in kind_a:
+        take("Y", 0, -2 if k % 2 == 0 else 2, k)
+    for (way, p, d, k) in [key for key in wire.ids if key[0] == "S"]:
+        take("S", p, d, k)
+    own.wait()
+    wire.drain()
+
+
+def gather_rows(features, nchunk=4, first_a=2, cid=1):
+    n = 4 * RING
+    return pl.pallas_call(
+        functools.partial(gather_kernel, nchunk, first_a),
+        out_shape=jax.ShapeDtypeStruct((n,) + features.shape, features.dtype),
+        in_specs=[pl.BlockSpec(memory_space=VM)],
+        out_specs=pl.BlockSpec(memory_space=ANY),
+        scratch_shapes=[pltpu.SemaphoreType.DMA((128,)), pltpu.SemaphoreType.DMA((128,)), pltpu.SemaphoreType.DMA],
+        compiler_params=pltpu.CompilerParams(collective_id=cid, has_side_effects=True, vmem_limit_bytes=48 << 20),
+        name="gather_rows",
+    )(features)
+
+
+def gelu_both(z):
+    c, a = 0.7978845608, 0.044715
+    z2 = z * z
+    t = jnp.tanh(c * (z + a * z * z2))
+    half = 0.5 * (1.0 + t)
+    slope = half + 0.5 * z * (1.0 - t * t) * (c * (1.0 + 3.0 * a * z2))
+    return z * half, slope
+
+
+def middle_kernel(nchunk, part, weight, gout, out, gh, gw,
+                  opp_in, t_out, in_r, in_l, s_out, y_in, gl, send_sem, recv_sem, own_sem):
+    blk, dev = col_place()
+    wire = Wire(send_sem, recv_sem)
+    rows = gout.shape[0] // nchunk
+    to = {"R": dev(0, 1), "L": dev(0, -1), "Y": dev(1, 0)}
+    barrier(list(to.values()))
+    cut = lambda k: pl.ds(k * rows, rows)
+    f = lambda v: v.astype(f32)
+    chunks = range(nchunk)
+    way_of = lambda k: "R" if k % 2 == 0 else "L"
+    side = {"R": 1, "L": -1}
+    arrive = {"R": in_r, "L": in_l}
+    other = {"R": "L", "L": "R"}
+
+    for k in chunks:
+        for p in (1, 0):
+            wire.push(("opp", p, k), part.at[blk(p, 2), cut(k)], opp_in.at[p, cut(k)], to[way_of(k)])
+    for k in chunks:
+        w = other[way_of(k)]
+        for p in (1, 0):
+            wire.push((w, p, k), part.at[blk(p, side[w]), cut(k)], arrive[w].at[p, cut(k)], to[w])
+
+    def stage2(k):
+        w = way_of(k)
+        for p in (1, 0):
+            wire.take(("opp", p, k), opp_in.at[p, cut(k)], to["Y"])
+            t_out[p, cut(k)] = (f(part[blk(p, side[w]), cut(k)]) + f(opp_in[p, cut(k)])).astype(bf16)
+            wire.push((w, p, k), t_out.at[p, cut(k)], arrive[w].at[p, cut(k)], to[w])
+
+    def ring_sum(p, k):
+        for w in "RL":
+            wire.take((w, p, k), arrive[w].at[p, cut(k)], to["Y"])
+        return f(part[blk(p, 0), cut(k)]) + f(in_r[p, cut(k)]) + f(in_l[p, cut(k)])
+
+    def stage3(k):
+        s_out[cut(k)] = ring_sum(1, k).astype(bf16)
+        wire.push(("y", k), s_out.at[cut(k)], y_in.at[cut(k)], to["Y"])
+
+    i0 = lax.broadcasted_iota(i32, (rows, rows), 0)
+    i1 = lax.broadcasted_iota(i32, (rows, rows), 1)
+    inside = i0 % BLOCK
+    node = i0 - inside + jnp.where(inside < BLOCK // 2, 2 * inside, 2 * inside - (BLOCK - 1))
+    order = (node == i1).astype(f32).astype(bf16)
+    locals_ = []
+
+    def stage4(k):
+        total = ring_sum(0, k)
+        wire.take(("y", k), y_in.at[cut(k)], to["Y"])
+        hidden = (total + f(y_in[cut(k)])).astype(bf16)
+        w = weight[...]
+        pre = jnp.dot(hidden, w, preferred_element_type=f32)
+        go = jnp.dot(order, gout[cut(k)], preferred_element_type=f32)
+        act, slope = gelu_both(pre)
+        gp = (go * slope).astype(bf16)
+        gl[cut(k)] = lax.dot_general(gp, w, (((1,), (1,)), ((), ())), preferred_element_type=f32).astype(bf16)
+        for way in "YRL":
+            wire.push(("g" + way, 0, 0, k), gl.at[cut(k)], gh.at[blk(0, 0), cut(k)], to[way])
+        own = pltpu.make_async_copy(gl.at[cut(k)], gh.at[blk(0, 0), cut(k)], own_sem.at[k])
+        own.start()
+        locals_.append(own)
+        out[cut(k)] = lax.dot_general(order, act.astype(bf16), (((0,), (0,)), ((), ())),
+                                      preferred_element_type=f32).astype(bf16)
+        term = lax.dot_general(hidden, gp, (((0,), (0,)), ((), ())), preferred_element_type=f32)
+        if k == 0:
+            gw[...] = term
+        else:
+            gw[...] += term
+
+    def stage5(k):
+        spot = gh.at[blk(1, 0), cut(k)]
+        wire.take(("gY", 0, 0, k), spot, to["Y"])
+        for way in "RL":
+            wire.push(("g" + way, 1, 0, k), spot, spot, to[way])
+
+    def stage6(k):
+        for p in (0, 1):
+            for way in "RL":
+                d = -side[way]
+                spot = gh.at[blk(p, d), cut(k)]
+                wire.take(("g" + way, p, 0, k), spot, to["Y"])
+                if way == way_of(k):
+                    wire.push(("g" + way, p, 1, k), spot, spot, to[way])
+
+    def stage7(k):
+        for p in (0, 1):
+            wire.take(("g" + way_of(k), p, 1, k), gh.at[blk(p, 2), cut(k)], to["Y"])
+
+    for k in chunks:
+        stage2(k)
+    stages = [stage3, stage4, stage5, stage6, stage7]
+    for tick in range(nchunk + len(stages) - 1):
+        for s, stage in enumerate(stages):
+            if 0 <= tick - s < nchunk:
+                stage(tick - s)
+    for own in locals_:
+        own.wait()
+    wire.drain()
+
+
+def middle(part, weight, gout, nchunk=4, cid=2):
+    rows, width = gout.shape
+    n = part.shape[0]
+    piece = lambda *lead: pltpu.VMEM(lead + (rows, width), bf16)
+    return pl.pallas_call(
+        functools.partial(middle_kernel, nchunk),
+        out_shape=[jax.ShapeDtypeStruct((rows, width), bf16),
+                   jax.ShapeDtypeStruct((n, rows, width), bf16),
+                   jax.ShapeDtypeStruct((width, width), f32)],
+        in_specs=[pl.BlockSpec(memory_space=VM)] * 3,
+        out_specs=[pl.BlockSpec(memory_space=VM), pl.BlockSpec(memory_space=ANY), pl.BlockSpec(memory_space=VM)],
+        scratch_shapes=[piece(2), piece(2), piece(2), piece(2), piece(), piece(), piece(),
+                        pltpu.SemaphoreType.DMA((128,)), pltpu.SemaphoreType.DMA((128,)),
+                        pltpu.SemaphoreType.DMA((nchunk,))],
+        compiler_params=pltpu.CompilerParams(collective_id=cid, has_side_effects=True, vmem_limit_bytes=48 << 20),
+        name="middle",
+    )(part, weight, gout)
+
+
+def last_kernel(nchunk, part, term, out, gw,
+                sib_in, opp_out, opp_in, d_out, t_out, in_r, in_l, s_out, y_in,
+                w_sib, w_half, w_row, w_col, w_sum, w_full, send_sem, recv_sem):
+    blk, dev, core = row_place()
+    cblk, cdev = col_place()
+    wire = Wire(send_sem, recv_sem)
+    rows = out.shape[0] // nchunk
+    to = {"R": dev(0, 1), "L": dev(0, -1), "Y": dev(1, 0), "S": dev(0, 0, 1)}
+    peers = [(p, d) for p in (0, 1) for d in range(RING) if (p, d) != (0, 0)]
+    barrier([to["S"]] + [dev(p, d) for p, d in peers] + [cdev(p, d) for p, d in peers])
+    cut = lambda k: pl.ds(k * rows, rows)
+    f = lambda v: v.astype(f32)
+    chunks = range(nchunk)
+    way_of = lambda k: "R" if k % 2 == 0 else "L"
+    side = {"R": 1, "L": -1}
+    arrive = {"R": in_r, "L": in_l}
+    other = {"R": "L", "L": "R"}
+    rel = lambda p, d: p * RING + d % RING
+
+    half = term.shape[0] // 2
+    ninth = half // (2 * RING)
+    hd = lambda c: pl.ds(pl.multiple_of(c * half, half), half)
+    seat = lambda p, d: blk(p, d) // 2
+    sd = lambda j: pl.ds(pl.multiple_of(j * ninth, ninth), ninth)
+    wire.push("w0", term.at[hd(1 - core)], w_sib, to["S"])
+
+    def sib(p, d, k):
+        wire.push(("s", rel(p, d), k), part.at[blk(p, d, 1), cut(k)], sib_in.at[rel(p, d), cut(k)], to["S"])
+
+    for k in chunks:
+        for p in (1, 0):
+            sib(p, 2, k)
+    for k in chunks:
+        for p in (1, 0):
+            sib(p, side[other[way_of(k)]], k)
+    for k in chunks:
+        for p in (1, 0):
+            sib(p, side[way_of(k)], k)
+    for k in chunks:
+        for p in (1, 0):
+            sib(p, 0, k)
+
+    def both(p, d, k):
+        wire.take(("s", rel(p, d), k), sib_in.at[rel(p, d), cut(k)], to["S"])
+        return f(part[blk(p, d), cut(k)]) + f(sib_in[rel(p, d), cut(k)])
+
+    for k in chunks:
+        for p in (1, 0):
+            opp_out[p, cut(k)] = both(p, 2, k).astype(bf16)
+            wire.push(("opp", p, k), opp_out.at[p, cut(k)], opp_in.at[p, cut(k)], to[way_of(k)])
+    for k in chunks:
+        w = other[way_of(k)]
+        for p in (1, 0):
+            d_out[p, cut(k)] = both(p, side[w], k).astype(bf16)
+            wire.push((w, p, k), d_out.at[p, cut(k)], arrive[w].at[p, cut(k)], to[w])
+
+    wire.take("w0", w_sib, to["S"])
+    w_half[...] = term[hd(core)] + w_sib[...]
+    for i, (p, d) in enumerate(peers):
+        wire.push(("w1", i), w_half.at[sd(seat(p, d))], w_row.at[i], dev(p, d))
+
+    def stage2(k):
+        w = way_of(k)
+        for p in (1, 0):
+            base = both(p, side[w], k)
+            wire.take(("opp", p, k), opp_in.at[p, cut(k)], to["Y"])
+            t_out[p, cut(k)] = (base + f(opp_in[p, cut(k)])).astype(bf16)
+            wire.push((w, p, k), t_out.at[p, cut(k)], arrive[w].at[p, cut(k)], to[w])
+
+    def ring_sum(p, k):
+        base = both(p, 0, k)
+        for w in "RL":
+            wire.take((w, p, k), arrive[w].at[p, cut(k)], to["Y"])
+        return base + f(in_r[p, cut(k)]) + f(in_l[p, cut(k)])
+
+    def stage3(k):
+        s_out[cut(k)] = ring_sum(1, k).astype(bf16)
+        wire.push(("y", k), s_out.at[cut(k)], y_in.at[cut(k)], to["Y"])
+
+    def stage4(k):
+        total = ring_sum(0, k)
+        wire.take(("y", k), y_in.at[cut(k)], to["Y"])
+        out[cut(k)] = (total + f(y_in[cut(k)])).astype(bf16)
+
+    for k in chunks:
+        stage2(k)
+        if k == 1:
+            mine = w_half[sd(seat(0, 0))]
+            for i, (p, d) in enumerate(peers):
+                wire.take(("w1", i), w_row.at[i], to["Y"])
+                mine = mine + w_row[i]
+            w_sum[...] = mine
+            here = cblk(0, 0)
+            w_col[here] = mine
+            for i, (p, d) in enumerate(peers):
+                wire.push(("w2", i), w_sum, w_col.at[here], cdev(p, d))
+    for i, (p, d) in enumerate(peers):
+        wire.take(("w2", i), w_col.at[cblk(p, -d)], to["Y"])
+    total = w_col[0]
+    for i in range(1, 2 * RING):
+        total = total + w_col[i]
+    spot = lambda p, d: pl.ds(pl.multiple_of(core * half + seat(p, d) * ninth, ninth), ninth)
+    w_full[spot(0, 0)] = total
+    for i, (p, d) in enumerate(peers):
+        wire.push(("w3", i), w_full.at[spot(0, 0)], w_full.at[spot(0, 0)], dev(p, d))
+    stages = [stage3, stage4]
+    for tick in range(nchunk + len(stages) - 1):
+        for s, stage in enumerate(stages):
+            if 0 <= tick - s < nchunk:
+                stage(tick - s)
+        if tick == 0:
+            for i, (p, d) in enumerate(peers):
+                wire.take(("w3", i), w_full.at[spot(p, -d)], to["Y"])
+            wire.push("w4", w_full.at[hd(core)], w_full.at[hd(core)], to["S"])
+    wire.take("w4", w_full.at[hd(1 - core)], to["S"])
+    gw[...] = w_full[...]
+    wire.drain()
+
+
+def last(part, term, nchunk=4, cid=3):
+    n, rows, width = part.shape
+    piece = lambda *lead: pltpu.VMEM(lead + (rows, width), bf16)
+    wrows = term.shape[0]
+    wf = lambda *lead: pltpu.VMEM(lead + (term.shape[1],), f32)
+    nine = wrows // (4 * RING)
+    return pl.pallas_call(
+        functools.partial(last_kernel, nchunk),
+        out_shape=[jax.ShapeDtypeStruct((rows, width), bf16), jax.ShapeDtypeStruct(term.shape, f32)],
+        in_specs=[pl.BlockSpec(memory_space=VM)] * 2,
+        out_specs=[pl.BlockSpec(memory_space=VM)] * 2,
+        scratch_shapes=[piece(n // 2), piece(2), piece(2), piece(2), piece(2), piece(2), piece(2), piece(), piece(),
+                        wf(wrows // 2), wf(wrows // 2), wf(2 * RING - 1, nine), wf(2 * RING, nine), wf(nine), wf(wrows),
+                        pltpu.SemaphoreType.DMA((160,)), pltpu.SemaphoreType.DMA((160,))],
+        compiler_params=pltpu.CompilerParams(collective_id=cid, has_side_effects=True, vmem_limit_bytes=48 << 20),
+        name="last",
+    )(part, term)
 
 
 def per_device(features, weight, grad_out, tile_rows, tile_cols, tile_values, tile_counts):
     nodes_dev, width = features.shape
     nr = nodes_dev * lax.axis_size("col") // BLOCK
     nc = nodes_dev * lax.axis_size("row") // BLOCK
-    source = lax.all_gather(features, "row", axis=0, tiled=True)
     *lists, tot = make_meta(tile_rows, tile_cols, tile_counts, nr, nc)
     m = relayout(tile_values)
-    part = spmm(fwd_kernel, lists[:3], tot, m, source, nr, "spmm_fwd")
-    hidden = lax.psum_scatter(part.reshape(-1, width), "col", scatter_dimension=0, tiled=True)
-    hidden = hidden.reshape(-1, 2, BLOCK // 2, width).swapaxes(1, 2).reshape(nodes_dev, width)
-    pre = jnp.dot(hidden, weight, preferred_element_type=f32)
-    output = activate(pre).astype(bf16)
-    grad_pre = jax.vjp(activate, pre)[1](grad_out.astype(f32))[0].astype(bf16)
-    term = jnp.einsum("nd,ne->de", hidden, grad_pre, preferred_element_type=f32)
-    grad_weight = lax.psum(term, ("row", "col"))
-    grad_local = jnp.einsum("ne,de->nd", grad_pre, weight, preferred_element_type=f32).astype(bf16)
-    grad_local = grad_local.reshape(-1, BLOCK // 2, 2, width).swapaxes(1, 2).reshape(nodes_dev, width)
-    grad_hidden = lax.all_gather(grad_local, "col", axis=0, tiled=True)
-    back = spmm(bwd_kernel, lists[3:], tot, m, grad_hidden, nc, "spmm_bwd")
-    grad_feat = lax.psum_scatter(back.reshape(-1, width), "row", scatter_dimension=0, tiled=True)
+    source = gather_rows(features)
+    part = spmm(fwd_kernel, lists[:3], tot, m, source.reshape(-1, width), nr, "spmm_fwd")
+    output, grad_hidden, term = middle(part.reshape(-1, nodes_dev, width), weight, grad_out)
+    back = spmm(bwd_kernel, lists[3:], tot, m, grad_hidden.reshape(-1, width), nc, "spmm_bwd")
+    grad_feat, grad_weight = last(back.reshape(-1, nodes_dev, width), term)
     return output, grad_feat, grad_weight
 
 

time: 455 us -> 218 us (0.48)
  waiting for transfers between devices: 375 us -> 0 us
  Pallas kernels: 45.1 us -> 203 us
  between operations: 14.5 us -> 1.46 us
    reduce_scatter x2 -> x0, waiting for transfers between devices: 159 us -> none  [the longest x1 88.2 us: per_device(): lax.psum_scatter(part.reshape(-1, width), 'col', scatter_dimension=0, til...]
    pallas_call x0 -> x3, Pallas kernels: none -> 143 us  [the longest x1 61 us: middle(): pl.pallas_call(functools.partial(middle_kernel, nchunk), out_shape=[jax.S...]
    psum x1 -> x0, waiting for transfers between devices: 123 us -> none  [per_device(): grad_weight = lax.psum(term, ('row', 'col'))]
    all_gather x2 -> x0, waiting for transfers between devices: 92.6 us -> none  [the longest x1 60.9 us: per_device(): grad_hidden = lax.all_gather(grad_local, 'col', axis=0, tiled=True)]
    pallas_call x2, Pallas kernels: 43.3 us -> 58.2 us  [spmm(): pl.pallas_call(functools.partial(kernel, tiles, unroll), out_shape=jax.Sh...]
    unnamed x20 -> x26, local copies, waits for them, and re-layouts: 9.67 us -> 7.94 us
  transfers between devices with their start and end apart: 5 -> 0, of which waited for: 5 -> 0; matrix products, arithmetic and copies ran while one was open for 2% -> 0% of each run, Pallas kernels for 6% -> 0%
where the time goes in v2:
time: 218 us; the launch traced here: 217 us
  Pallas kernels  203 us (93%)
  local copies, waits for them, and re-layouts  12.5 us (6%)
    pallas_call x1, Pallas kernels, middle(): pl.pallas_call(functools.partial(middle_kernel, nchunk), out_shape=[jax.S...  61 us
    pallas_call x2, Pallas kernels, spmm(): pl.pallas_call(functools.partial(kernel, tiles, unroll), out_shape=jax.Sh...  58.2 us
    pallas_call x1, Pallas kernels, last(): pl.pallas_call(functools.partial(last_kernel, nchunk), out_shape=[jax.Sha...  51.6 us
    pallas_call x1, Pallas kernels, gather_rows(): pl.pallas_call(functools.partial(gather_kernel, nchunk, first_a), out_sha...  30.9 us
    unnamed x26, local copies, waits for them, and re-layouts  7.94 us

profile of v2, /device:TPU:0, one launch (start us, length us, event | category | flops | bytes accessed | tf_op | source)
XLA Modules:
  0.0 217.4 jit_solution(9450598286823689906)
XLA Ops:
  1.3 0.7 pad.8.rows_ref
  2.0 0.7 pad.9.cols_ref
  2.7 1.8 meta.1
  4.4 0.0 copy-start.4
  4.4 0.0 copy-start.5
  4.4 0.0 copy-start.6
  4.5 0.0 copy-start.7
  4.5 0.0 copy-start.8
  4.5 0.0 copy-start.9
  4.5 0.0 copy-start.10
  4.5 3.9 %copy.10 = bf16[76,8,32,128]{3,2,1,0:T(8,128)(2,1)S(1)} copy(bf16[76,8,32,128]{3,1,2,0:T(8,128)(2,1)} %bitcast.15) | data formatting | bytes 9961472
  8.5 0.0 copy-done.4
  8.5 0.0 copy-done.5
  8.5 0.0 copy-done.6
  8.5 0.0 copy-done.7
  8.5 0.0 copy-done.8
  8.5 0.0 copy-done.9
  8.5 0.0 copy-done.10
  8.5 0.0 copy-start.1
  8.5 3.2 %concatenate.3.m_ref = bf16[609,32,128]{2,1,0:T(8,128)(2,1)} pad(bf16[608,32,128]{2,1,0:T(8,128)(2,1)S(1)} %bitcast.13, bf16[]{:T(256)} %constant.1.clone.1), padding=0_1x0_0x0_0 | pad | bytes 9969666 | tf_op jit(solution)/shard_map/concatenate | solution.py:152
  11.7 0.0 copy-done.1
  11.7 30.9 %gather_rows.1 = bf16[16,768,256]{2,1,0:T(8,128)(2,1)} custom-call(bf16[768,256]{1,0:T(8,128)(2,1)S(1)} %copy-done.1), custom_call_target="tpu_custom_call" | custom-call | tf_op jit(solution)/shard_map/gather_rows/pallas_call | solution.py:285
  42.6 0.0 copy-start.2
  42.6 0.0 copy-start.3
  42.6 26.9 %spmm_fwd.1 = bf16[96,64,256]{2,1,0:T(8,128)(2,1)} custom-call(s32[1,128]{1,0:T(1,128)} %copy-done.8, s32[1,1024]{1,0:T(1,128)} %copy-done.6, s32[1,1024]{1,0:T(1,128)} %copy-done.7, s32[1,256]{1,0:T(1,128)} %copy-done.10, bf16[609,32,128]{2,1,0:T(8,128)(2,1)} %concatenate.3.m_ref, bf16[192,64,256]{2,1,0:T(8,128)(2,1)} %bitcast.12), custom_call_target="tpu_custom_call" | custom-call | tf_op jit(solution)/shard_map/spmm_fwd/pallas_call | solution.py:138
  69.5 61.0 %middle.1 = (bf16[768,256]{1,0:T(8,128)(2,1)S(1)}, bf16[8,768,256]{2,1,0:T(8,128)(2,1)S(1)}, f32[256,256]{1,0:T(8,128)S(1)}) custom-call(bf16[8,768,256]{2,1,0:T(8,128)(2,1)} %bitcast.14, bf16[256,256]{1,0:T(8,128)(2,1)S(1)} %copy-done.3, bf16[768,256]{1,0:T(8,128)(2,1)S(1)} %copy-done.2), custom_call_target="tpu_custom_call" | custom-call | tf_op jit(solution)/shard_map/middle/pallas_call | solution.py:409
  130.5 1.7 copy-done
  132.3 31.3 %spmm_bwd.1 = bf16[192,64,256]{2,1,0:T(8,128)(2,1)} custom-call(s32[1,128]{1,0:T(1,128)} %copy-done.8, s32[1,1536]{1,0:T(1,128)} %copy-done.4, s32[1,1536]{1,0:T(1,128)} %copy-done.5, s32[1,384]{1,0:T(1,128)} %copy-done.9, bf16[609,32,128]{2,1,0:T(8,128)(2,1)} %concatenate.3.m_ref, bf16[96,64,256]{2,1,0:T(8,128)(2,1)} %bitcast.10), custom_call_target="tpu_custom_call" | custom-call | tf_op jit(solution)/shard_map/spmm_bwd/pallas_call | solution.py:138
  163.6 51.6 %last.1 = (bf16[768,256]{1,0:T(8,128)(2,1)S(1)}, f32[256,256]{1,0:T(8,128)S(1)}) custom-call(bf16[16,768,256]{2,1,0:T(8,128)(2,1)} %bitcast.11, f32[256,256]{1,0:T(8,128)S(1)} %get-tuple-element.24.term), custom_call_target="tpu_custom_call" | custom-call | tf_op jit(solution)/shard_map/last/pallas_call | solution.py:549
  215.2 0.7 copy.15
  215.9 0.7 copy.16
  216.7 0.7 copy.17
  (3 shorter events, 0.0 us)
Async XLA Ops:
  4.4 4.0 %copy-start.4 = (s32[1,1536]{1,0:T(1,128)}, s32[1,1536]{1,0:T(1,128)S(1)}, u32[]{:S(2)}) copy-start(s32[1,1536]{1,0:T(1,128)S(1)} %get-tuple-element.20.t_ref) | copy-start | bytes 18436
  4.4 4.0 %copy-start.5 = (s32[1,1536]{1,0:T(1,128)}, s32[1,1536]{1,0:T(1,128)S(1)}, u32[]{:S(2)}) copy-start(s32[1,1536]{1,0:T(1,128)S(1)} %get-tuple-element.21.o_ref) | copy-start | bytes 18436
  4.4 4.0 %copy-start.6 = (s32[1,1024]{1,0:T(1,128)}, s32[1,1024]{1,0:T(1,128)S(1)}, u32[]{:S(2)}) copy-start(s32[1,1024]{1,0:T(1,128)S(1)} %get-tuple-element.16.t_ref) | copy-start | bytes 12292
  4.5 4.0 %copy-start.7 = (s32[1,1024]{1,0:T(1,128)}, s32[1,1024]{1,0:T(1,128)S(1)}, u32[]{:S(2)}) copy-start(s32[1,1024]{1,0:T(1,128)S(1)} %get-tuple-element.17.o_ref) | copy-start | bytes 12292
  4.5 4.0 %copy-start.8 = (s32[1,128]{1,0:T(1,128)}, s32[1,128]{1,0:T(1,128)S(1)}, u32[]{:S(2)}) copy-start(s32[1,128]{1,0:T(1,128)S(1)} %get-tuple-element.15.tot_ref) | copy-start | bytes 1540
  4.5 4.0 %copy-start.9 = (s32[1,384]{1,0:T(1,128)}, s32[1,384]{1,0:T(1,128)S(1)}, u32[]{:S(2)}) copy-start(s32[1,384]{1,0:T(1,128)S(1)} %get-tuple-element.22.b_ref) | copy-start | bytes 4612
  4.5 4.0 %copy-start.10 = (s32[1,256]{1,0:T(1,128)}, s32[1,256]{1,0:T(1,128)S(1)}, u32[]{:S(2)}) copy-start(s32[1,256]{1,0:T(1,128)S(1)} %get-tuple-element.18.b_ref) | copy-start | bytes 3076
  8.5 3.2 %copy-start.1 = (bf16[768,256]{1,0:T(8,128)(2,1)S(1)}, bf16[768,256]{1,0:T(8,128)(2,1)}, u32[]{:S(2)}) copy-start(bf16[768,256]{1,0:T(8,128)(2,1)} %feat.1) | copy-start | bytes 1179652
  42.6 26.9 %copy-start.2 = (bf16[768,256]{1,0:T(8,128)(2,1)S(1)}, bf16[768,256]{1,0:T(8,128)(2,1)}, u32[]{:S(2)}) copy-start(bf16[768,256]{1,0:T(8,128)(2,1)} %gout.1) | copy-start | bytes 1179652
  42.6 26.9 %copy-start.3 = (bf16[256,256]{1,0:T(8,128)(2,1)S(1)}, bf16[256,256]{1,0:T(8,128)(2,1)}, u32[]{:S(2)}) copy-start(bf16[256,256]{1,0:T(8,128)(2,1)} %weight.1) | copy-start | bytes 393220
  130.5 1.8 copy-start

commit v3 on v2

--- a/solution.py
+++ b/solution.py
@@ -132,7 +132,7 @@
         out_ref[s * 8:s * 8 + 8] = acc[s * 8:s * 8 + 8].astype(bf16)
 
 
-def spmm(kernel, meta3, tot, m, src, nb, name, unroll=2):
+def spmm(kernel, meta3, tot, m, src, nb, name, unroll=16):
     tiles = m.shape[0]
     width = src.shape[1]
     return pl.pallas_call(
@@ -209,7 +209,7 @@
     return blk, (lambda p, d: {"col": blk(p, d)})
 
 
-def gather_kernel(nchunk, first_a, feat, out, send_sem, recv_sem, own_sem):
+def gather_kernel(nchunk, first_a, feat, values, out, m_out, send_sem, recv_sem, own_sem):
     blk, dev, _ = row_place()
     wire = Wire(send_sem, recv_sem)
     rows = feat.shape[0] // nchunk
@@ -251,6 +251,11 @@
         push("L", 0, 0, k)
     for k in kind_b + kind_a:
         push("S", 0, 0, k)
+    tiles = values.shape[0]
+
+    for s in range(0, tiles, 16):
+        m_out[s:s + 16] = values[s:s + 16].reshape((16,) + m_out.shape[1:])
+    m_out[tiles:] = jnp.zeros((1,) + m_out.shape[1:], bf16)
     for k in kind_b:
         take("Y", 0, 0, k)
     for k in kind_a:
@@ -280,17 +285,18 @@
     wire.drain()
 
 
-def gather_rows(features, nchunk=4, first_a=2, cid=1):
+def gather_rows(features, values, nchunk=4, first_a=2, cid=1):
     n = 4 * RING
     return pl.pallas_call(
         functools.partial(gather_kernel, nchunk, first_a),
-        out_shape=jax.ShapeDtypeStruct((n,) + features.shape, features.dtype),
-        in_specs=[pl.BlockSpec(memory_space=VM)],
-        out_specs=pl.BlockSpec(memory_space=ANY),
+        out_shape=[jax.ShapeDtypeStruct((n,) + features.shape, features.dtype),
+                   jax.ShapeDtypeStruct((values.shape[0] + 1, BLOCK // 2, 2 * BLOCK), bf16)],
+        in_specs=[pl.BlockSpec(memory_space=VM)] * 2,
+        out_specs=[pl.BlockSpec(memory_space=ANY), pl.BlockSpec(memory_space=VM)],
         scratch_shapes=[pltpu.SemaphoreType.DMA((128,)), pltpu.SemaphoreType.DMA((128,)), pltpu.SemaphoreType.DMA],
         compiler_params=pltpu.CompilerParams(collective_id=cid, has_side_effects=True, vmem_limit_bytes=48 << 20),
         name="gather_rows",
-    )(features)
+    )(features, values)
 
 
 def gelu_both(z):
@@ -564,8 +570,7 @@
     nr = nodes_dev * lax.axis_size("col") // BLOCK
     nc = nodes_dev * lax.axis_size("row") // BLOCK
     *lists, tot = make_meta(tile_rows, tile_cols, tile_counts, nr, nc)
-    m = relayout(tile_values)
-    source = gather_rows(features)
+    source, m = gather_rows(features, tile_values.reshape(tile_values.shape[2:]))
     part = spmm(fwd_kernel, lists[:3], tot, m, source.reshape(-1, width), nr, "spmm_fwd")
     output, grad_hidden, term = middle(part.reshape(-1, nodes_dev, width), weight, grad_out)
     back = spmm(bwd_kernel, lists[3:], tot, m, grad_hidden.reshape(-1, width), nc, "spmm_bwd")

time: 218 us -> 188 us (0.86)
  Pallas kernels: 203 us -> 174 us
    pallas_call x2, Pallas kernels: 58.2 us -> 24.3 us  [spmm(): pl.pallas_call(functools.partial(kernel, tiles, unroll), out_shape=jax.Sh...]
    concatenate x1 -> x0, local copies, waits for them, and re-layouts: 3.19 us -> none  [relayout(): return jnp.concatenate([m, jnp.zeros((1, 32, 128), bf16)], axis=0)]
    pallas_call x1, Pallas kernels: 61 us -> 63.9 us  [middle(): pl.pallas_call(functools.partial(middle_kernel, nchunk), out_shape=[jax.S...]
    pallas_call x1, Pallas kernels: 30.9 us -> 33.2 us  [gather_rows(): pl.pallas_call(functools.partial(gather_kernel, nchunk, first_a), out_sha...]
    unnamed x26 -> x27, local copies, waits for them, and re-layouts: 7.94 us -> 10.2 us
where the time goes in v3:
time: 188 us; the launch traced here: 187 us
  Pallas kernels  174 us (93%)
  local copies, waits for them, and re-layouts  11.6 us (6%)
    pallas_call x1, Pallas kernels, middle(): pl.pallas_call(functools.partial(middle_kernel, nchunk), out_shape=[jax.S...  63.9 us
    pallas_call x1, Pallas kernels, last(): pl.pallas_call(functools.partial(last_kernel, nchunk), out_shape=[jax.Sha...  51.3 us
    pallas_call x1, Pallas kernels, gather_rows(): pl.pallas_call(functools.partial(gather_kernel, nchunk, first_a), out_sha...  33.2 us
    pallas_call x2, Pallas kernels, spmm(): pl.pallas_call(functools.partial(kernel, tiles, unroll), out_shape=jax.Sh...  24.3 us
    unnamed x27, local copies, waits for them, and re-layouts  10.2 us

profile of v3, /device:TPU:0, one launch (start us, length us, event | category | flops | bytes accessed | tf_op | source)
XLA Modules:
  0.0 187.4 jit_solution(17725470451137875624)
XLA Ops:
  1.3 0.7 pad.7.rows_ref
  2.0 0.7 pad.8.cols_ref
  2.7 1.8 meta.1
  4.4 0.0 copy-start.6
  4.4 0.6 copy-done.6
  5.0 0.0 copy-start.8
  5.0 0.6 copy-done.8
  5.6 0.0 copy-start.10
  5.6 0.5 copy-done.10
  6.1 0.0 copy-start.11
  6.1 0.6 copy-done.11
  6.7 0.0 copy-start.5
  6.7 0.0 copy-start.7
  6.7 0.6 copy-done.5
  7.3 0.0 copy-done.7
  7.3 0.0 copy-done.9
  7.3 2.4 %copy-done = bf16[1,1,608,4096]{3,2,1,0:T(8,128)(2,1)S(1)} copy-done((bf16[1,1,608,4096]{3,2,1,0:T(8,128)(2,1)S(1)}, bf16[1,1,608,4096]{3,2,1,0:T(8,128)(2,1)}, u32[]{:S(2)}) %copy-start) | copy-done | bytes 4980760
  9.7 1.0 copy-done.3
  10.7 33.2 %gather_rows.1 = (bf16[16,768,256]{2,1,0:T(8,128)(2,1)}, bf16[609,32,128]{2,1,0:T(8,128)(2,1)}) custom-call(bf16[768,256]{1,0:T(8,128)(2,1)S(1)} %copy-done.3, bf16[608,4096]{1,0:T(8,128)(2,1)S(1)} %bitcast.7), custom_call_target="tpu_custom_call" | custom-call | tf_op jit(solution)/shard_map/gather_rows/pallas_call | solution.py:290
  43.9 0.0 copy-start.2
  43.9 0.0 copy-start.4
  43.9 11.2 %spmm_fwd.1 = bf16[96,64,256]{2,1,0:T(8,128)(2,1)} custom-call(s32[1,128]{1,0:T(1,128)} %copy-done.9, s32[1,1024]{1,0:T(1,128)} %copy-done.7, s32[1,1024]{1,0:T(1,128)} %copy-done.8, s32[1,256]{1,0:T(1,128)} %copy-done.11, bf16[609,32,128]{2,1,0:T(8,128)(2,1)} %get-tuple-element.21.m_ref, bf16[192,64,256]{2,1,0:T(8,128)(2,1)} %bitcast.11), custom_call_target="tpu_custom_call" | custom-call | tf_op jit(solution)/shard_map/spmm_fwd/pallas_call | solution.py:138
  55.2 0.0 copy-done.2
  55.2 0.0 copy-done.4
  55.2 63.9 %middle.1 = (bf16[768,256]{1,0:T(8,128)(2,1)S(1)}, bf16[8,768,256]{2,1,0:T(8,128)(2,1)S(1)}, f32[256,256]{1,0:T(8,128)S(1)}) custom-call(bf16[8,768,256]{2,1,0:T(8,128)(2,1)} %bitcast.10, bf16[256,256]{1,0:T(8,128)(2,1)S(1)} %copy-done.4, bf16[768,256]{1,0:T(8,128)(2,1)S(1)} %copy-done.2), custom_call_target="tpu_custom_call" | custom-call | tf_op jit(solution)/shard_map/middle/pallas_call | solution.py:415
  119.1 0.0 copy-start.1
  119.1 1.7 copy-done.1
  120.8 13.0 %spmm_bwd.1 = bf16[192,64,256]{2,1,0:T(8,128)(2,1)} custom-call(s32[1,128]{1,0:T(1,128)} %copy-done.9, s32[1,1536]{1,0:T(1,128)} %copy-done.5, s32[1,1536]{1,0:T(1,128)} %copy-done.6, s32[1,384]{1,0:T(1,128)} %copy-done.10, bf16[609,32,128]{2,1,0:T(8,128)(2,1)} %get-tuple-element.21.m_ref, bf16[96,64,256]{2,1,0:T(8,128)(2,1)} %bitcast.8), custom_call_target="tpu_custom_call" | custom-call | tf_op jit(solution)/shard_map/spmm_bwd/pallas_call | solution.py:138
  133.9 51.3 %last.1 = (bf16[768,256]{1,0:T(8,128)(2,1)S(1)}, f32[256,256]{1,0:T(8,128)S(1)}) custom-call(bf16[16,768,256]{2,1,0:T(8,128)(2,1)} %bitcast.9, f32[256,256]{1,0:T(8,128)S(1)} %get-tuple-element.28.term), custom_call_target="tpu_custom_call" | custom-call | tf_op jit(solution)/shard_map/last/pallas_call | solution.py:555
  185.2 0.7 copy.14
  186.0 0.7 copy.15
  186.7 0.7 copy.16
  (3 shorter events, 0.0 us)
Async XLA Ops:
  4.4 0.6 copy-start.6
  5.0 0.6 copy-start.8
  5.6 0.5 copy-start.10
  6.1 0.6 copy-start.11
  6.7 0.6 copy-start.5
  6.7 0.6 copy-start.7
  6.7 0.6 copy-start.9
  7.3 2.4 %copy-start = (bf16[1,1,608,4096]{3,2,1,0:T(8,128)(2,1)S(1)}, bf16[1,1,608,4096]{3,2,1,0:T(8,128)(2,1)}, u32[]{:S(2)}) copy-start(bf16[1,1,608,4096]{3,2,1,0:T(8,128)(2,1)} %param.12) | copy-start | bytes 14942212
  9.7 1.0 copy-start.3
  43.9 11.3 %copy-start.2 = (bf16[768,256]{1,0:T(8,128)(2,1)S(1)}, bf16[768,256]{1,0:T(8,128)(2,1)}, u32[]{:S(2)}) copy-start(bf16[768,256]{1,0:T(8,128)(2,1)} %gout.1) | copy-start | bytes 1179652
  43.9 11.2 %copy-start.4 = (bf16[256,256]{1,0:T(8,128)(2,1)S(1)}, bf16[256,256]{1,0:T(8,128)(2,1)}, u32[]{:S(2)}) copy-start(bf16[256,256]{1,0:T(8,128)(2,1)} %weight.1) | copy-start | bytes 393220
  119.1 1.7 copy-start.1

commit v4 on v0

v4 whole, which is shorter than its diff:
```python
import functools

import jax
import jax.numpy as jnp
from jax import lax
from jax.experimental import pallas as pl
from jax.experimental.pallas import tpu as pltpu
from jax.sharding import PartitionSpec as P

BLOCK = 64
GROUP = 4
UNROLL = 16
RING = 4
LANES = 128
MESH = pl.DeviceIdType.MESH
VM = pltpu.VMEM
f32, bf16, i32 = jnp.float32, jnp.bfloat16, jnp.int32


def up(n, m):
    return -(-n // m) * m


def group_bound(tiles, blocks):
    return up((tiles + (GROUP - 1) * min(blocks, tiles)) // GROUP, UNROLL)


def lists_of(key_row, other_row, tiles, nb, groups_max, wide):
    tp = key_row.shape[1]
    nbp = up(nb, LANES)
    hot = (lax.broadcasted_iota(i32, (nbp, tp), 0) == key_row).astype(f32)
    hotb = hot.astype(bf16)
    count = jnp.sum(hot, axis=1, keepdims=True)
    upper = (lax.broadcasted_iota(i32, (tp, tp), 0) < lax.broadcasted_iota(i32, (tp, tp), 1)).astype(f32).astype(bf16)
    rank = jnp.dot(hotb, upper, preferred_element_type=f32)
    groups = jnp.floor((count + (GROUP - 1)) * (1.0 / GROUP))
    b0 = lax.broadcasted_iota(i32, (nbp, nbp), 0)
    b1 = lax.broadcasted_iota(i32, (nbp, nbp), 1)
    lower = (b1 < b0).astype(f32).astype(bf16)
    first = jnp.dot(lower, jnp.broadcast_to(groups, (nbp, LANES)).astype(bf16), preferred_element_type=f32)[:, :1]
    place = jnp.sum(hot * (rank + GROUP * first), axis=0, keepdims=True)
    live = jnp.sum(hot, axis=0, keepdims=True) > 0
    place = jnp.where(live, place, -1.0).astype(i32)
    spot = (lax.broadcasted_iota(i32, (wide, tp), 0) == place).astype(f32).astype(bf16)
    t = lax.broadcasted_iota(i32, (1, tp), 1)
    row = lax.broadcasted_iota(i32, (8, tp), 0)
    data = jnp.where(row == 0, t // 128, jnp.where(row == 1, t % 128, jnp.where(row == 2, other_row, 1)))
    got = lax.dot_general(data.astype(f32).astype(bf16), spot, (((1,), (1,)), ((), ())), preferred_element_type=f32)
    there = got[3:4] > 0
    tile = jnp.where(there, got[0:1] * 128 + got[1:2], float(tiles)).astype(i32)
    other = jnp.where(there, got[2:3], 0.0).astype(i32)
    g = lax.broadcasted_iota(i32, (nbp, wide), 1).astype(f32)
    starts = jnp.sum(jnp.where(jnp.logical_and(first == g, groups > 0), 1.0, 0.0), axis=0, keepdims=True).astype(i32)
    last = jnp.where(groups > 0, first + groups - 1, float(groups_max))
    last = jnp.sum(jnp.where(b0 == b1, last, 0.0), axis=0, keepdims=True).astype(i32)
    last = jnp.concatenate([last, jnp.zeros((1, wide - nbp), i32)], axis=1)
    return [tile, other, starts, last]


def lists_kernel(tiles, nr, nc, wide, rows_ref, cols_ref, count_ref, out_ref, keep):
    tp = keep.shape[1]
    keep[...] = jnp.zeros_like(keep)
    keep[0:1, :tiles] = rows_ref[...]
    keep[1:2, :tiles] = cols_ref[...]
    live = lax.broadcasted_iota(i32, (1, tp), 1) < count_ref[0, 0]
    rows, cols = keep[0:1], keep[1:2]
    fwd = lists_of(jnp.where(live, rows, 4096), cols, tiles, nr, group_bound(tiles, nr), wide)
    bwd = lists_of(jnp.where(live, cols, 4096), rows, tiles, nc, group_bound(tiles, nc), wide)
    for i, v in enumerate(fwd + bwd):
        out_ref[i:i + 1] = v


def make_lists(rows, cols, count, nr, nc):
    tiles = rows.shape[-1]
    wide = up(GROUP * max(group_bound(tiles, nr), group_bound(tiles, nc)), LANES)
    return pl.pallas_call(
        functools.partial(lists_kernel, tiles, nr, nc, wide),
        out_shape=jax.ShapeDtypeStruct((8, wide), i32),
        in_specs=[pl.BlockSpec(memory_space=VM)] * 2 + [pl.BlockSpec(memory_space=pltpu.SMEM)],
        out_specs=pl.BlockSpec(memory_space=VM),
        scratch_shapes=[pltpu.VMEM((8, up(tiles, LANES)), i32)],
        compiler_params=pltpu.CompilerParams(vmem_limit_bytes=48 << 20),
        name="lists",
    )(rows.reshape(1, tiles), cols.reshape(1, tiles), count)


class Wire:
    def __init__(self, send_sem, recv_sem):
        self.send_sem, self.recv_sem = send_sem, recv_sem
        self.ids, self.sent = {}, []

    def _sems(self, key):
        n = self.ids.setdefault(key, len(self.ids))
        assert n < self.send_sem.shape[0]
        return dict(send_sem=self.send_sem.at[n], recv_sem=self.recv_sem.at[n])

    def push(self, key, src, dst, dev):
        copy = pltpu.make_async_remote_copy(
            src_ref=src, dst_ref=dst, device_id=dev, device_id_type=MESH, **self._sems(key))
        copy.start()
        self.sent.append(copy)

    def take(self, key, dst, dev):
        pltpu.make_async_remote_copy(
            src_ref=dst, dst_ref=dst, device_id=dev, device_id_type=MESH, **self._sems(key)).wait_recv()

    def drain(self):
        for copy in self.sent:
            copy.wait_send()


def barrier(devs):
    sem = pltpu.get_barrier_semaphore()
    for dev in devs:
        pl.semaphore_signal(sem, inc=1, device_id=dev, device_id_type=MESH)
    pl.semaphore_wait(sem, len(devs))


def row_place():
    r = lax.axis_index("row")
    pair, ring, core = r // (2 * RING), (r // 2) % RING, r % 2

    def blk(p, d, s=0):
        return (pair + p) % 2 * (2 * RING) + (ring + d) % RING * 2 + (core + s) % 2

    return blk, (lambda p, d, s=0: {"row": blk(p, d, s)}), core


def col_place():
    c = lax.axis_index("col")
    pair, ring = c // RING, c % RING

    def blk(p, d):
        return (pair + p) % 2 * RING + (ring + d) % RING

    return blk, (lambda p, d: {"col": blk(p, d)})


def gelu_both(z):
    c, a = 0.7978845608, 0.044715
    z2 = z * z
    t = jnp.tanh(c * (z + a * z * z2))
    half = 0.5 * (1.0 + t)
    slope = half + 0.5 * z * (1.0 - t * t) * (c * (1.0 + 3.0 * a * z2))
    return z * half, slope


def swap_halves(m):
    return jnp.concatenate([m[:, BLOCK:], m[:, :BLOCK]], axis=1)


def weave(work, steps):
    done = 0
    for i, piece in enumerate(work):
        piece()
        goal = len(steps) * (i + 1) // len(work)
        while done < goal:
            steps[done]()
            done += 1


def step_of(fn, *args):
    return lambda: fn(*args)


def layer_kernel(lists, feat, values, weight, gout, out, gfeat, gw,
                 vals, m, src_0, src_1, runs, part,
                 c_opp, c_t, c_r, c_l, c_s, c_y, hid, gl, gh_0, gh_1, back,
                 sib_in, o_out, o_in, d_out, t_out, in_r, in_l, s_out, y_in,
                 term, w_sib, w_half, w_row, w_col, w_sum, w_full,
                 send_sem, recv_sem, val_sem):
    rblk, rdev, core = row_place()
    cblk, cdev = col_place()
    wire = Wire(send_sem, recv_sem)
    peers = [(p, d) for p in (0, 1) for d in range(RING) if (p, d) != (0, 0)]
    load = pltpu.make_async_copy(values, vals, val_sem)
    load.start()
    barrier([rdev(0, 0, 1)] + [rdev(p, d) for p, d in peers] + [cdev(p, d) for p, d in peers])

    f = lambda v: v.astype(f32)
    src, gh = (src_0, src_1), (gh_0, gh_1)
    tiles = vals.shape[0]
    nbd = feat.shape[0] // BLOCK
    nr, nc = part.shape[1], src_0.shape[0]
    gf, gb = group_bound(tiles, nr), group_bound(tiles, nc)
    row_to = {"R": rdev(0, 1), "L": rdev(0, -1), "Y": rdev(1, 0), "S": rdev(0, 0, 1)}
    col_to = {"R": cdev(0, 1), "L": cdev(0, -1), "Y": cdev(1, 0)}
    any_dev = row_to["S"]
    side = {"R": 1, "L": -1}
    other = {"R": "L", "L": "R"}

    cb = nbd // 2

    def gather(h):
        def slot(p, d, s, k, part_):
            size = cb if part_ is None else cb // 2
            at = rblk(p, d, s) * nbd + k * cb + (0 if part_ is None else part_ * size)
            return src[h].at[pl.ds(at, size)]

        def push(way, p, d, k, part_=None):
            spot = slot(p, d, 0, k, part_)
            wire.push(("f", h, way, p, d % RING, k, part_), spot, spot, row_to[way])

        def take(way, p, d, k, part_=None):
            key = ("f", h, way, p, d % RING, k, part_)
            if way == "S":
                wire.take(key, slot(p, d, 1, k, part_), any_dev)
                return
            q, e = {"R": (p, d - 1), "L": (p, d + 1), "Y": (1 - p, d)}[way]
            wire.take(key, slot(q, e, 0, k, part_), any_dev)
            if way == "Y":
                if k == 1:
                    push("R", q, e, k)
                    push("L", q, e, k)
            else:
                if abs(e) == 1:
                    push(way, q, e, k, 0 if way == "R" else 1)
                if k == 0:
                    push("Y", q, e, k, part_)
            push("S", q, e, k, part_)

        def own():
            here = pl.ds(rblk(0, 0) * nbd, nbd)
            src[h][here] = feat[:, h * LANES:(h + 1) * LANES].reshape(nbd, BLOCK, LANES)
            for k in (1, 0):
                for way in "YRL":
                    push(way, 0, 0, k)
            for k in (1, 0):
                push("S", 0, 0, k)

        order = [("Y", 0, 0, 1), ("R", 0, 0, 0), ("L", 0, 0, 0), ("Y", 0, 0, 0), ("R", 0, 0, 1), ("L", 0, 0, 1),
                 ("R", 0, -1, 0, 0), ("L", 0, 1, 0, 1), ("R", 1, 0, 1), ("L", 1, 0, 1),
                 ("Y", 0, -1, 0), ("Y", 0, 1, 0)]
        order += [("R", p, -1, 1, 0) if way == "R" else ("L", p, 1, 1, 1) for p in (0, 1) for way in "RL"]
        order += [("Y", 0, -2, 0, 0), ("Y", 0, 2, 0, 1)]
        steps = [step_of(take, *o) for o in order]

        def close():
            for key in [key for key in wire.ids if key[:3] == ("f", h, "S")]:
                take("S", *key[3:])

        return own, steps + [close]

    low = lax.broadcasted_iota(i32, (BLOCK // 2, 2 * BLOCK), 1) < BLOCK

    def lhs_fwd(g):
        v = [m[lists[0, g * GROUP + k]] for k in range(GROUP)]
        s = [swap_halves(x) for x in v]
        even = [jnp.where(low, v[0], s[1]), jnp.where(low, v[2], s[3])]
        odd = [jnp.where(low, s[0], v[1]), jnp.where(low, s[2], v[3])]
        return jnp.concatenate([jnp.concatenate(even, axis=1), jnp.concatenate(odd, axis=1)], axis=0)

    def rhs_fwd(h, g):
        return jnp.concatenate([src[h][lists[1, g * GROUP + k]] for k in range(GROUP)], axis=0)

    def lhs_bwd(g):
        w = jnp.concatenate([m[lists[4, g * GROUP + k]] for k in range(GROUP)], axis=0).T
        return jnp.concatenate([w[:BLOCK], w[BLOCK:]], axis=1)

    def rhs_bwd(h, g):
        v = [gh[h][lists[5, g * GROUP + k]] for k in range(GROUP)]
        return jnp.concatenate([x[:BLOCK // 2] for x in v] + [x[BLOCK // 2:] for x in v], axis=0)

    def products(h, lhs, rhs, flags, groups, pieces):
        state = [jnp.zeros((BLOCK, LANES), f32)]
        turns = groups // UNROLL

        def body(i, run):
            prods = []
            for u in range(UNROLL):
                g = i * UNROLL + u
                prods.append((g, jnp.dot(lhs(g), rhs(h, g), preferred_element_type=f32)))
            for g, p in prods:
                run = jnp.where(lists[flags, g] > 0, p, run + p)
                runs[g] = run.astype(bf16)
            return run

        def piece(i):
            lo, hi = turns * i // pieces, turns * (i + 1) // pieces
            state[0] = lax.fori_loop(lo, hi, body, state[0])

        return [step_of(piece, i) for i in range(pieces)]

    def settle(dst, h, lasts, groups, blocks):
        runs[groups] = jnp.zeros((BLOCK, LANES), bf16)

        def body(i, _):
            for u in range(8):
                dst[h, i * 8 + u] = runs[lists[lasts, i * 8 + u]]
            return 0

        lax.fori_loop(0, blocks // 8, body, 0)

    nk = 4
    ck = nbd // nk
    chunks = range(nk)
    way_of = lambda k: "R" if k % 2 == 0 else "L"
    cut = lambda k: pl.ds(k * ck, ck)
    blk_cut = lambda b, k: pl.ds(b * nbd + k * ck, ck)
    c_in = {"R": c_r, "L": c_l}

    def c_start(h):
        for k in chunks:
            for p in (1, 0):
                wire.push(("c", h, "opp", p, k), part.at[h, blk_cut(cblk(p, 2), k)], c_opp.at[h, p, cut(k)], col_to[way_of(k)])
        for k in chunks:
            w = other[way_of(k)]
            for p in (1, 0):
                wire.push(("c", h, w, p, k), part.at[h, blk_cut(cblk(p, side[w]), k)], c_in[w].at[h, p, cut(k)], col_to[w])

    def c_ring(h, k):
        w = way_of(k)
        for p in (1, 0):
            wire.take(("c", h, "opp", p, k), c_opp.at[h, p, cut(k)], any_dev)
            c_t[h, p, cut(k)] = (f(part[h, blk_cut(cblk(p, side[w]), k)]) + f(c_opp[h, p, cut(k)])).astype(bf16)
            wire.push(("c", h, w, p, k), c_t.at[h, p, cut(k)], c_in[w].at[h, p, cut(k)], col_to[w])

    def c_sum(h, p, k):
        for w in "RL":
            wire.take(("c", h, w, p, k), c_in[w].at[h, p, cut(k)], any_dev)
        return f(part[h, blk_cut(cblk(p, 0), k)]) + f(c_r[h, p, cut(k)]) + f(c_l[h, p, cut(k)])

    def c_pair(h, k):
        c_s[h, cut(k)] = c_sum(h, 1, k).astype(bf16)
        wire.push(("c", h, "y", k), c_s.at[h, cut(k)], c_y.at[h, cut(k)], col_to["Y"])

    def c_end(h, k):
        total = c_sum(h, 0, k)
        wire.take(("c", h, "y", k), c_y.at[h, cut(k)], any_dev)
        hid[h, cut(k)] = (total + f(c_y[h, cut(k)])).astype(bf16)

    rows = ck * BLOCK
    i0 = lax.broadcasted_iota(i32, (rows, rows), 0)
    i1 = lax.broadcasted_iota(i32, (rows, rows), 1)
    inside = i0 % BLOCK
    node = i0 - inside + jnp.where(inside < BLOCK // 2, 2 * inside, 2 * inside - (BLOCK - 1))
    order = (node == i1).astype(f32).astype(bf16)

    def g_push(h, k):
        for way in "YRL":
            wire.push(("g", h, way, 0, 0, k), gl.at[h, cut(k)], gh[h].at[blk_cut(cblk(0, 0), k)], col_to[way])

    def dense(k):
        hidden = jnp.concatenate([hid[h, cut(k)].reshape(rows, LANES) for h in (0, 1)], axis=1)
        w = weight[...]
        at = pl.ds(k * rows, rows)
        pre = jnp.dot(hidden, w, preferred_element_type=f32)
        go = jnp.dot(order, gout[at], preferred_element_type=f32)
        act, slope = gelu_both(pre)
        gp = (go * slope).astype(bf16)
        local = lax.dot_general(gp, w, (((1,), (1,)), ((), ())), preferred_element_type=f32).astype(bf16)
        for h in (0, 1):
            mine = local[:, h * LANES:(h + 1) * LANES].reshape(ck, BLOCK, LANES)
            gl[h, cut(k)] = mine
        g_push(0, k)
        for h in (0, 1):
            gh[h][blk_cut(cblk(0, 0), k)] = gl[h, cut(k)]
        out[at] = lax.dot_general(order, act.astype(bf16), (((0,), (0,)), ((), ())),
                                  preferred_element_type=f32).astype(bf16)
        t = lax.dot_general(hidden, gp, (((0,), (0,)), ((), ())), preferred_element_type=f32)
        if k == 0:
            term[...] = t
        else:
            term[...] += t

    def g_pair(h, k):
        spot = gh[h].at[blk_cut(cblk(1, 0), k)]
        wire.take(("g", h, "Y", 0, 0, k), spot, any_dev)
        for way in "RL":
            wire.push(("g", h, way, 1, 0, k), spot, spot, col_to[way])

    def g_ring(h, k):
        for p in (0, 1):
            for way in "RL":
                spot = gh[h].at[blk_cut(cblk(p, -side[way]), k)]
                wire.take(("g", h, way, p, 0, k), spot, any_dev)
                if way == way_of(k):
                    wire.push(("g", h, way, p, 1, k), spot, spot, col_to[way])

    def g_far(h, k):
        for p in (0, 1):
            wire.take(("g", h, way_of(k), p, 1, k), gh[h].at[blk_cut(cblk(p, 2), k)], any_dev)

    r_in = {"R": in_r, "L": in_l}
    rel = lambda p, d: p * RING + d % RING
    arrived = set()

    def r_start(h):
        for d in (2, 1, -1, 0):
            for p in (1, 0):
                there = pl.ds(rblk(p, d, 1) * nbd, nbd)
                wire.push(("s", h, rel(p, d)), back.at[h, there], sib_in.at[h, rel(p, d)], row_to["S"])

    def both(h, p, d, k):
        key = ("s", h, rel(p, d))
        if key not in arrived:
            arrived.add(key)
            wire.take(key, sib_in.at[h, rel(p, d)], any_dev)
        return f(back[h, blk_cut(rblk(p, d), k)]) + f(sib_in[h, rel(p, d), cut(k)])

    def r_far(h, k):
        for p in (1, 0):
            o_out[h, p, cut(k)] = both(h, p, 2, k).astype(bf16)
            wire.push(("r", h, "opp", p, k), o_out.at[h, p, cut(k)], o_in.at[h, p, cut(k)], row_to[way_of(k)])

    def r_near(h, k):
        w = other[way_of(k)]
        for p in (1, 0):
            d_out[h, p, cut(k)] = both(h, p, side[w], k).astype(bf16)
            wire.push(("r", h, w, p, k), d_out.at[h, p, cut(k)], r_in[w].at[h, p, cut(k)], row_to[w])

    def r_ring(h, k):
        w = way_of(k)
        for p in (1, 0):
            base = both(h, p, side[w], k)
            wire.take(("r", h, "opp", p, k), o_in.at[h, p, cut(k)], any_dev)
            t_out[h, p, cut(k)] = (base + f(o_in[h, p, cut(k)])).astype(bf16)
            wire.push(("r", h, w, p, k), t_out.at[h, p, cut(k)], r_in[w].at[h, p, cut(k)], row_to[w])

    def r_sum(h, p, k):
        base = both(h, p, 0, k)
        for w in "RL":
            wire.take(("r", h, w, p, k), r_in[w].at[h, p, cut(k)], any_dev)
        return base + f(in_r[h, p, cut(k)]) + f(in_l[h, p, cut(k)])

    def r_pair(h, k):
        s_out[h, cut(k)] = r_sum(h, 1, k).astype(bf16)
        wire.push(("r", h, "y", k), s_out.at[h, cut(k)], y_in.at[h, cut(k)], row_to["Y"])

    def r_end(h, k):
        total = r_sum(h, 0, k)
        wire.take(("r", h, "y", k), y_in.at[h, cut(k)], any_dev)
        total = (total + f(y_in[h, cut(k)])).astype(bf16)
        gfeat[pl.ds(k * rows, rows), h * LANES:(h + 1) * LANES] = total.reshape(rows, LANES)

    def pipeline(stages, n):
        return [step_of(stage, k) for tick in range(n + len(stages) - 1)
                for s, stage in enumerate(stages) for k in [tick - s] if 0 <= k < n]

    def r_steps(h):
        steps = [step_of(r_far, h, k) for k in chunks] + [step_of(r_near, h, k) for k in chunks]
        steps += [step_of(r_ring, h, k) for k in chunks]
        return steps + pipeline([lambda k: r_pair(h, k), lambda k: r_end(h, k)], nk)

    half = term.shape[0] // 2
    eighth = half // (2 * RING)
    hd = lambda c: pl.ds(pl.multiple_of(c * half, half), half)
    seat = lambda p, d: rblk(p, d) // 2
    sd = lambda j: pl.ds(pl.multiple_of(j * eighth, eighth), eighth)
    spot_of = lambda p, d: pl.ds(pl.multiple_of(core * half + seat(p, d) * eighth, eighth), eighth)

    def w0():
        wire.push("w0", term.at[hd(1 - core)], w_sib, row_to["S"])

    def w1():
        wire.take("w0", w_sib, any_dev)
        w_half[...] = term[hd(core)] + w_sib[...]
        for i, (p, d) in enumerate(peers):
            wire.push(("w1", i), w_half.at[sd(seat(p, d))], w_row.at[i], rdev(p, d))

    def w2():
        mine = w_half[sd(seat(0, 0))]
        for i, _ in enumerate(peers):
            wire.take(("w1", i), w_row.at[i], any_dev)
            mine = mine + w_row[i]
        w_sum[...] = mine
        here = cblk(0, 0)
        w_col[here] = mine
        for i, (p, d) in enumerate(peers):
            wire.push(("w2", i), w_sum, w_col.at[here], cdev(p, d))

    def w3():
        for i, (p, d) in enumerate(peers):
            wire.take(("w2", i), w_col.at[cblk(p, -d)], any_dev)
        total = w_col[0]
        for i in range(1, 2 * RING):
            total = total + w_col[i]
        w_full[spot_of(0, 0)] = total
        for i, (p, d) in enumerate(peers):
            wire.push(("w3", i), w_full.at[spot_of(0, 0)], w_full.at[spot_of(0, 0)], rdev(p, d))

    def w4():
        for i, (p, d) in enumerate(peers):
            wire.take(("w3", i), w_full.at[spot_of(p, -d)], any_dev)
        wire.push("w4", w_full.at[hd(core)], w_full.at[hd(core)], row_to["S"])

    def w5():
        wire.take("w4", w_full.at[hd(1 - core)], any_dev)
        gw[...] = w_full[...]

    own0, steps0 = gather(0)
    own1, steps1 = gather(1)
    own0()
    load.wait()
    for s in range(0, tiles, 16):
        m[s:s + 16] = vals[s:s + 16].reshape((16,) + m.shape[1:])
    m[tiles:] = jnp.zeros((1,) + m.shape[1:], bf16)
    for i, step in enumerate(steps0):
        step()
        if i == 5:
            own1()
    weave(products(0, lhs_fwd, rhs_fwd, 2, gf, 7), steps1[:-1])
    settle(part, 0, 3, gf, nr)
    c_start(0)
    steps1[-1]()
    c_steps = [step_of(c_ring, 0, k) for k in chunks]
    c_steps += pipeline([lambda k: c_pair(0, k), lambda k: c_end(0, k)], nk)
    weave(products(1, lhs_fwd, rhs_fwd, 2, gf, 7), c_steps)
    settle(part, 1, 3, gf, nr)
    c_start(1)
    for k in chunks:
        c_ring(1, k)
    def finish(k):
        c_end(1, k)
        dense(k)

    for step in pipeline([lambda k: c_pair(1, k), finish, lambda k: g_pair(0, k)], nk):
        step()
    for k in chunks:
        g_push(1, k)
    w0()
    for step in pipeline([lambda k: g_ring(0, k), lambda k: g_far(0, k)], nk):
        step()
    g_steps = [step_of(g_pair, 1, k) for k in chunks] + [w1] + [step_of(g_ring, 1, k) for k in chunks] + [w2]
    g_steps += [step_of(g_far, 1, k) for k in chunks] + [w3]
    weave(products(0, lhs_bwd, rhs_bwd, 6, gb, 9), g_steps)
    settle(back, 0, 7, gb, nc)
    r_start(0)
    weave(products(1, lhs_bwd, rhs_bwd, 6, gb, 9), r_steps(0) + [w4])
    settle(back, 1, 7, gb, nc)
    r_start(1)
    for step in r_steps(1):
        step()
    w5()
    wire.drain()


def layer(lists, features, values, weight, grad_out, nr, nc):
    rows, width = features.shape
    tiles = values.shape[0]
    nbd = rows // BLOCK
    gmax = max(group_bound(tiles, nr), group_bound(tiles, nc))
    wrows = weight.shape[0]
    piece = lambda *lead: pltpu.VMEM(lead + (BLOCK, LANES), bf16)
    wf = lambda *lead: pltpu.VMEM(lead + (wrows,), f32)
    eighth = wrows // (4 * RING)
    two = 2
    scratch = [
        pltpu.VMEM(values.shape, bf16), pltpu.VMEM((tiles + 1, BLOCK // 2, 2 * BLOCK), bf16),
        piece(nc), piece(nc), piece(gmax + 1), piece(two, nr),
        piece(two, 2, nbd), piece(two, 2, nbd), piece(two, 2, nbd), piece(two, 2, nbd),
        piece(two, nbd), piece(two, nbd), piece(two, nbd), piece(two, nbd), piece(nr), piece(nr), piece(two, nc),
        piece(two, 2 * RING, nbd), piece(two, 2, nbd), piece(two, 2, nbd), piece(two, 2, nbd), piece(two, 2, nbd),
        piece(two, 2, nbd), piece(two, 2, nbd), piece(two, nbd), piece(two, nbd),
        wf(wrows), wf(wrows // 2), wf(wrows // 2), wf(2 * RING - 1, eighth), wf(2 * RING, eighth), wf(eighth), wf(wrows),
        pltpu.SemaphoreType.DMA((400,)), pltpu.SemaphoreType.DMA((400,)), pltpu.SemaphoreType.DMA,
    ]
    return pl.pallas_call(
        layer_kernel,
        out_shape=[jax.ShapeDtypeStruct((rows, width), bf16), jax.ShapeDtypeStruct((rows, width), bf16),
                   jax.ShapeDtypeStruct((wrows, width), f32)],
        in_specs=[pl.BlockSpec(memory_space=pltpu.SMEM), pl.BlockSpec(memory_space=VM), pl.BlockSpec(memory_space=pl.ANY),
                  pl.BlockSpec(memory_space=VM), pl.BlockSpec(memory_space=VM)],
        out_specs=[pl.BlockSpec(memory_space=VM)] * 3,
        scratch_shapes=scratch,
        compiler_params=pltpu.CompilerParams(collective_id=1, has_side_effects=True, vmem_limit_bytes=60 << 20),
        name="layer",
    )(lists, features, values, weight, grad_out)


def per_device(features, weight, grad_out, tile_rows, tile_cols, tile_values, tile_counts):
    nodes_dev = features.shape[0]
    nr = nodes_dev * lax.axis_size("col") // BLOCK
    nc = nodes_dev * lax.axis_size("row") // BLOCK
    lists = make_lists(tile_rows, tile_cols, tile_counts, nr, nc)
    values = tile_values.reshape(tile_values.shape[2:])
    return tuple(layer(lists, features, values, weight, grad_out, nr, nc))


def solution(mesh):
    placed = (
        P(("col", "row"), None),
        P(),
        P(("row", "col"), None),
        P("row", "col", None),
        P("row", "col", None),
        P("row", "col", None, None),
        P("row", "col"),
    )
    return jax.shard_map(
        per_device,
        mesh=mesh,
        in_specs=placed,
        out_specs=(P(("row", "col"), None), P(("col", "row"), None), P()),
        check_vma=False,
    )
```

time: 787 us -> 175 us (0.22)
  other arithmetic: 283 us -> 0 us
  waiting for transfers between devices: 250 us -> 0 us
  Pallas kernels: 0 us -> 165 us
  local copies, waits for them, and re-layouts: 169 us -> 7.18 us
  matrix products: 66.2 us -> 0 us
  between operations: 13.8 us -> 1.32 us
    scatter-add x8 -> x0, other arithmetic: 263 us -> none  [step(): return total.at[put_now].add(product)]
    pallas_call x0 -> x2, Pallas kernels: none -> 165 us  [the longest x1 163 us: layer(): pl.pallas_call(layer_kernel, out_shape=[jax.ShapeDtypeStruct((rows, width...]
    reduce_scatter x2 -> x0, waiting for transfers between devices: 151 us -> none  [the longest x1 81.4 us: per_device(): lax.psum_scatter(partial_value.astype(jnp.bfloat16), 'col', scatter_dimen...]
    all_gather x2 -> x0, waiting for transfers between devices: 98.2 us -> none  [the longest x1 60.7 us: per_device(): grad_hidden = lax.all_gather(grad_local, 'col', axis=0, tiled=True)]
    gather x8 -> x0, local copies, waits for them, and re-layouts: 80.1 us -> none  [step(): picked = pieces[take_now]]
    dynamic_slice x16 -> x0, local copies, waits for them, and re-layouts: 69.8 us -> none  [step(): chosen = lax.dynamic_slice_in_dim(blocks, start, group, 0)]
    dot_general x11 -> x0, matrix products: 66.2 us -> none  [the longest x4 30.9 us: step(): jnp.einsum('tij,tjd->tid', chosen, picked, preferred_element_type=jnp.flo...]
    convert_element_type x2 -> x0, other arithmetic: 13.1 us -> none  [the longest x1 8.18 us: per_device(): backward.astype(jnp.bfloat16)]
  transfers between devices with their start and end apart: 5 -> 0, of which waited for: 4 -> 0; matrix products, arithmetic and copies ran while one was open for 34% -> 0% of each run, Pallas kernels for 0% -> 0%
where the time goes in v4:
time: 175 us; the launch traced here: 174 us
  Pallas kernels  165 us (94%)
  local copies, waits for them, and re-layouts  7.18 us (4%)
    pallas_call x1, Pallas kernels, layer(): pl.pallas_call(layer_kernel, out_shape=[jax.ShapeDtypeStruct((rows, width...  163 us
    unnamed x9, local copies, waits for them, and re-layouts  7.18 us

profile of v4, /device:TPU:0, one launch (start us, length us, event | category | flops | bytes accessed | tf_op | source)
XLA Modules:
  0.0 174.0 jit_solution(4785851104867635103)
XLA Ops:
  1.3 0.0 copy-start.1
  1.3 0.7 copy-done.1
  2.0 0.0 copy-start.2
  2.0 0.7 copy-done.2
  2.6 2.0 %lists.1 = s32[8,1280]{1,0:T(8,128)S(1)} custom-call(s32[1,608]{1,0:T(1,128)S(1)} %bitcast.3, s32[1,608]{1,0:T(1,128)S(1)} %bitcast.4, s32[1,1]{1,0:T(1,128)S(6)} %copy.13.count_ref), custom_call_target="tpu_custom_call" | custom-call | tf_op jit(solution)/shard_map/lists/pallas_call | solution.py:76
  4.7 0.0 copy-start
  4.7 0.6 copy-done
  5.3 163.4 %layer.1 = (bf16[768,256]{1,0:T(8,128)(2,1)}, bf16[768,256]{1,0:T(8,128)(2,1)}, f32[256,256]{1,0:T(8,128)}) custom-call(s32[8,1280]{1,0:T(8,128)} %copy-done, bf16[768,256]{1,0:T(8,128)(2,1)} %feat.1, bf16[608,4096]{1,0:T(8,128)(2,1)} %bitcast.5, bf16[256,256]{1,0:T(8,128)(2,1)} %weight.1, bf16[768,256]{1,0:T(8,128)(2,1)} %gout.1), custom_call_target="tpu_custom_call" | custom-call | tf_op jit(solution)/shard_map/layer/pallas_call | solution.py:558
  168.8 1.8 %copy.14 = bf16[768,256]{1,0:T(8,128)(2,1)} copy(bf16[768,256]{1,0:T(8,128)(2,1)} %get-tuple-element.6) | data formatting | bytes 786432
  170.5 1.8 %copy.15 = bf16[768,256]{1,0:T(8,128)(2,1)} copy(bf16[768,256]{1,0:T(8,128)(2,1)} %get-tuple-element.7) | data formatting | bytes 786432
  172.3 1.7 copy.16
Async XLA Ops:
  1.3 0.7 copy-start.1
  2.0 0.7 copy-start.2
  4.7 0.6 copy-start

commit v5 on v4

--- a/solution.py
+++ b/solution.py
@@ -57,13 +57,18 @@
     return [tile, other, starts, last]
 
 
-def lists_kernel(tiles, nr, nc, wide, rows_ref, cols_ref, count_ref, out_ref, keep):
-    tp = keep.shape[1]
+def lists_kernel(tiles, nr, nc, rows_in, cols_in, count_ref, out_ref, t_rows, t_cols, keep, sems):
+    loads = [pltpu.make_async_copy(rows_in, t_rows, sems.at[0]), pltpu.make_async_copy(cols_in, t_cols, sems.at[1])]
+    for load in loads:
+        load.start()
     keep[...] = jnp.zeros_like(keep)
-    keep[0:1, :tiles] = rows_ref[...]
-    keep[1:2, :tiles] = cols_ref[...]
-    live = lax.broadcasted_iota(i32, (1, tp), 1) < count_ref[0, 0]
+    for load in loads:
+        load.wait()
+    wide = out_ref.shape[1]
+    keep[0:1, :tiles] = t_rows[0]
+    keep[1:2, :tiles] = t_cols[0]
     rows, cols = keep[0:1], keep[1:2]
+    live = lax.broadcasted_iota(i32, rows.shape, 1) < count_ref[0, 0]
     fwd = lists_of(jnp.where(live, rows, 4096), cols, tiles, nr, group_bound(tiles, nr), wide)
     bwd = lists_of(jnp.where(live, cols, 4096), rows, tiles, nc, group_bound(tiles, nc), wide)
     for i, v in enumerate(fwd + bwd):
@@ -74,14 +79,15 @@
     tiles = rows.shape[-1]
     wide = up(GROUP * max(group_bound(tiles, nr), group_bound(tiles, nc)), LANES)
     return pl.pallas_call(
-        functools.partial(lists_kernel, tiles, nr, nc, wide),
+        functools.partial(lists_kernel, tiles, nr, nc),
         out_shape=jax.ShapeDtypeStruct((8, wide), i32),
-        in_specs=[pl.BlockSpec(memory_space=VM)] * 2 + [pl.BlockSpec(memory_space=pltpu.SMEM)],
+        in_specs=[pl.BlockSpec(memory_space=pl.ANY)] * 2 + [pl.BlockSpec(memory_space=pltpu.SMEM)],
         out_specs=pl.BlockSpec(memory_space=VM),
-        scratch_shapes=[pltpu.VMEM((8, up(tiles, LANES)), i32)],
-        compiler_params=pltpu.CompilerParams(vmem_limit_bytes=48 << 20),
+        scratch_shapes=[pltpu.VMEM(rows.shape, i32), pltpu.VMEM(cols.shape, i32), pltpu.VMEM((8, up(tiles, LANES)), i32),
+                        pltpu.SemaphoreType.DMA((2,))],
+        compiler_params=pltpu.CompilerParams(vmem_limit_bytes=60 << 20),
         name="lists",
-    )(rows.reshape(1, tiles), cols.reshape(1, tiles), count)
+    )(rows, cols, count)
 
 
 class Wire:
@@ -109,11 +115,11 @@
             copy.wait_send()
 
 
-def barrier(devs):
+def greet(devs):
     sem = pltpu.get_barrier_semaphore()
     for dev in devs:
         pl.semaphore_signal(sem, inc=1, device_id=dev, device_id_type=MESH)
-    pl.semaphore_wait(sem, len(devs))
+    return lambda: pl.semaphore_wait(sem, len(devs))
 
 
 def row_place():
@@ -149,33 +155,24 @@
     return jnp.concatenate([m[:, BLOCK:], m[:, :BLOCK]], axis=1)
 
 
-def weave(work, steps):
-    done = 0
-    for i, piece in enumerate(work):
-        piece()
-        goal = len(steps) * (i + 1) // len(work)
-        while done < goal:
-            steps[done]()
-            done += 1
-
-
 def step_of(fn, *args):
     return lambda: fn(*args)
 
 
-def layer_kernel(lists, feat, values, weight, gout, out, gfeat, gw,
-                 vals, m, src_0, src_1, runs, part,
-                 c_opp, c_t, c_r, c_l, c_s, c_y, hid, gl, gh_0, gh_1, back,
-                 sib_in, o_out, o_in, d_out, t_out, in_r, in_l, s_out, y_in,
+def layer_kernel(lists, feat_in, weight_in, gout_in, values_in, out, gfeat, gw,
+                 feat, weight, gout, vals, m, src_0, src_1, runs, part,
+                 c_bufs, hid, gl, gh_0, gh_1, back, sib_in, r_bufs,
                  term, w_sib, w_half, w_row, w_col, w_sum, w_full,
-                 send_sem, recv_sem, val_sem):
+                 send_sem, recv_sem, load_sem):
     rblk, rdev, core = row_place()
     cblk, cdev = col_place()
     wire = Wire(send_sem, recv_sem)
     peers = [(p, d) for p in (0, 1) for d in range(RING) if (p, d) != (0, 0)]
-    load = pltpu.make_async_copy(values, vals, val_sem)
-    load.start()
-    barrier([rdev(0, 0, 1)] + [rdev(p, d) for p, d in peers] + [cdev(p, d) for p, d in peers])
+    met = greet([rdev(0, 0, 1)] + [rdev(p, d) for p, d in peers] + [cdev(p, d) for p, d in peers])
+    loads = [pltpu.make_async_copy(a, b, load_sem.at[i]) for i, (a, b) in enumerate([
+        (feat_in, feat), (values_in, vals), (weight_in, weight), (gout_in, gout)])]
+    for load in loads:
+        load.start()
 
     f = lambda v: v.astype(f32)
     src, gh = (src_0, src_1), (gh_0, gh_1)
@@ -220,20 +217,29 @@
             push("S", q, e, k, part_)
 
         def own():
-            here = pl.ds(rblk(0, 0) * nbd, nbd)
-            src[h][here] = feat[:, h * LANES:(h + 1) * LANES].reshape(nbd, BLOCK, LANES)
-            for k in (1, 0):
-                for way in "YRL":
+            push("Y", 0, 0, 1)
+            for k in (0, 1):
+                for way in "RL":
                     push(way, 0, 0, k)
-            for k in (1, 0):
+            for k in (0, 1):
                 push("S", 0, 0, k)
 
-        order = [("Y", 0, 0, 1), ("R", 0, 0, 0), ("L", 0, 0, 0), ("Y", 0, 0, 0), ("R", 0, 0, 1), ("L", 0, 0, 1),
+        def own_late():
+            push("Y", 0, 0, 0)
+
+        order = [("Y", 0, 0, 1), ("R", 0, 0, 0), ("L", 0, 0, 0), ("R", 0, 0, 1), ("L", 0, 0, 1),
                  ("R", 0, -1, 0, 0), ("L", 0, 1, 0, 1), ("R", 1, 0, 1), ("L", 1, 0, 1),
-                 ("Y", 0, -1, 0), ("Y", 0, 1, 0)]
+                 ("Y", 0, 0, 0), ("Y", 0, -1, 0), ("Y", 0, 1, 0)]
         order += [("R", p, -1, 1, 0) if way == "R" else ("L", p, 1, 1, 1) for p in (0, 1) for way in "RL"]
         order += [("Y", 0, -2, 0, 0), ("Y", 0, 2, 0, 1)]
         steps = [step_of(take, *o) for o in order]
+        first = steps[2]
+
+        def third():
+            first()
+            own_late()
+
+        steps[2] = third
 
         def close():
             for key in [key for key in wire.ids if key[:3] == ("f", h, "S")]:
@@ -294,40 +300,102 @@
     nk = 4
     ck = nbd // nk
     chunks = range(nk)
+    kind_a, kind_b = chunks[:1], chunks[1:]
+    ca = len(kind_a) * ck
     way_of = lambda k: "R" if k % 2 == 0 else "L"
     cut = lambda k: pl.ds(k * ck, ck)
     blk_cut = lambda b, k: pl.ds(b * nbd + k * ck, ck)
-    c_in = {"R": c_r, "L": c_l}
-
-    def c_start(h):
-        for k in chunks:
-            for p in (1, 0):
-                wire.push(("c", h, "opp", p, k), part.at[h, blk_cut(cblk(p, 2), k)], c_opp.at[h, p, cut(k)], col_to[way_of(k)])
-        for k in chunks:
+
+    class Sums:
+        def __init__(self, tag, to, base, ref, bufs):
+            self.tag, self.to, self.base, self.ref = tag, to, base, ref
+            (self.ya_out, self.ya_in, self.o_out, self.o_in, self.n_out, self.t_out,
+             self.r_in, self.l_in, self.s_out, self.y_in) = bufs
+            self.inn = {"R": self.r_in, "L": self.l_in}
+            self.got = set()
+
+        def ya(self, h, d):
+            if self.ref is not None:
+                spot = self.ref(h, 1, d, None)
+            else:
+                for k in kind_a:
+                    self.ya_out[h, d % RING, cut(k)] = self.base(h, 1, d, k).astype(bf16)
+                spot = self.ya_out.at[h, d % RING, pl.ds(0, ca)]
+            wire.push((self.tag, h, "ya", d % RING), spot, self.ya_in.at[h, d % RING, pl.ds(0, ca)], self.to["Y"])
+
+        def term(self, h, p, d, k):
+            if k in kind_b:
+                return self.base(h, p, d, k)
+            key = (self.tag, h, "ya", d % RING)
+            if key not in self.got:
+                self.got.add(key)
+                wire.take(key, self.ya_in.at[h, d % RING, pl.ds(0, ca)], any_dev)
+            return self.base(h, 0, d, k) + f(self.ya_in[h, d % RING, cut(k)])
+
+        def ps(self, k):
+            return (0,) if k in kind_a else (1, 0)
+
+        def _out(self, h, p, d, k, buf):
+            if self.ref is not None and k in kind_b:
+                return self.ref(h, p, d, k)
+            buf[h, p, cut(k)] = self.term(h, p, d, k).astype(bf16)
+            return buf.at[h, p, cut(k)]
+
+        def far(self, h, k):
+            for p in self.ps(k):
+                wire.push((self.tag, h, "opp", p, k), self._out(h, p, 2, k, self.o_out), self.o_in.at[h, p, cut(k)],
+                          self.to[way_of(k)])
+
+        def near(self, h, k):
             w = other[way_of(k)]
-            for p in (1, 0):
-                wire.push(("c", h, w, p, k), part.at[h, blk_cut(cblk(p, side[w]), k)], c_in[w].at[h, p, cut(k)], col_to[w])
-
-    def c_ring(h, k):
-        w = way_of(k)
-        for p in (1, 0):
-            wire.take(("c", h, "opp", p, k), c_opp.at[h, p, cut(k)], any_dev)
-            c_t[h, p, cut(k)] = (f(part[h, blk_cut(cblk(p, side[w]), k)]) + f(c_opp[h, p, cut(k)])).astype(bf16)
-            wire.push(("c", h, w, p, k), c_t.at[h, p, cut(k)], c_in[w].at[h, p, cut(k)], col_to[w])
-
-    def c_sum(h, p, k):
-        for w in "RL":
-            wire.take(("c", h, w, p, k), c_in[w].at[h, p, cut(k)], any_dev)
-        return f(part[h, blk_cut(cblk(p, 0), k)]) + f(c_r[h, p, cut(k)]) + f(c_l[h, p, cut(k)])
-
-    def c_pair(h, k):
-        c_s[h, cut(k)] = c_sum(h, 1, k).astype(bf16)
-        wire.push(("c", h, "y", k), c_s.at[h, cut(k)], c_y.at[h, cut(k)], col_to["Y"])
+            for p in self.ps(k):
+                wire.push((self.tag, h, w, p, k), self._out(h, p, side[w], k, self.n_out), self.inn[w].at[h, p, cut(k)],
+                          self.to[w])
+
+        def ring(self, h, k):
+            w = way_of(k)
+            for p in self.ps(k):
+                own = self.term(h, p, side[w], k)
+                wire.take((self.tag, h, "opp", p, k), self.o_in.at[h, p, cut(k)], any_dev)
+                self.t_out[h, p, cut(k)] = (own + f(self.o_in[h, p, cut(k)])).astype(bf16)
+                wire.push((self.tag, h, w, p, k), self.t_out.at[h, p, cut(k)], self.inn[w].at[h, p, cut(k)], self.to[w])
+
+        def total(self, h, p, k):
+            own = self.term(h, p, 0, k)
+            for w in "RL":
+                wire.take((self.tag, h, w, p, k), self.inn[w].at[h, p, cut(k)], any_dev)
+            return own + f(self.r_in[h, p, cut(k)]) + f(self.l_in[h, p, cut(k)])
+
+        def pair(self, h, k):
+            if k in kind_b:
+                self.s_out[h, cut(k)] = self.total(h, 1, k).astype(bf16)
+                wire.push((self.tag, h, "y", k), self.s_out.at[h, cut(k)], self.y_in.at[h, cut(k)], self.to["Y"])
+
+        def end(self, h, k):
+            value = self.total(h, 0, k)
+            if k in kind_b:
+                wire.take((self.tag, h, "y", k), self.y_in.at[h, cut(k)], any_dev)
+                value = value + f(self.y_in[h, cut(k)])
+            return value.astype(bf16)
+
+        def begin(self, h):
+            return ([step_of(self.ya, h, 2)] + [step_of(self.far, h, k) for k in kind_b]
+                    + [step_of(self.ya, h, d) for d in (1, -1)] + [step_of(self.near, h, k) for k in kind_b]
+                    + [step_of(self.ya, h, 0)])
+
+        def second(self, h):
+            return [step_of(self.far, h, k) for k in kind_a] + [step_of(self.near, h, k) for k in kind_a]
+
+    def c_base(h, p, d, k):
+        return f(part[h, blk_cut(cblk(p, d), k)])
+
+    def c_ref(h, p, d, k):
+        return part.at[h, pl.ds(cblk(p, d) * nbd, ca) if k is None else blk_cut(cblk(p, d), k)]
+
+    cs = Sums("c", col_to, c_base, c_ref, c_bufs)
 
     def c_end(h, k):
-        total = c_sum(h, 0, k)
-        wire.take(("c", h, "y", k), c_y.at[h, cut(k)], any_dev)
-        hid[h, cut(k)] = (total + f(c_y[h, cut(k)])).astype(bf16)
+        hid[h, cut(k)] = cs.end(h, k)
 
     rows = ck * BLOCK
     i0 = lax.broadcasted_iota(i32, (rows, rows), 0)
@@ -339,6 +407,10 @@
     def g_push(h, k):
         for way in "YRL":
             wire.push(("g", h, way, 0, 0, k), gl.at[h, cut(k)], gh[h].at[blk_cut(cblk(0, 0), k)], col_to[way])
+
+    def g_pass(h, p, d, k, way, hop):
+        spot = gh[h].at[blk_cut(cblk(p, d), k)]
+        wire.push(("g", h, way, p, hop, k), spot, spot, col_to[way])
 
     def dense(k):
         hidden = jnp.concatenate([hid[h, cut(k)].reshape(rows, LANES) for h in (0, 1)], axis=1)
@@ -364,83 +436,52 @@
             term[...] += t
 
     def g_pair(h, k):
-        spot = gh[h].at[blk_cut(cblk(1, 0), k)]
-        wire.take(("g", h, "Y", 0, 0, k), spot, any_dev)
-        for way in "RL":
-            wire.push(("g", h, way, 1, 0, k), spot, spot, col_to[way])
+        wire.take(("g", h, "Y", 0, 0, k), gh[h].at[blk_cut(cblk(1, 0), k)], any_dev)
+        if k in kind_b:
+            for way in "RL":
+                g_pass(h, 1, 0, k, way, 0)
 
     def g_ring(h, k):
-        for p in (0, 1):
+        for p in (0,) if k in kind_a else (0, 1):
             for way in "RL":
-                spot = gh[h].at[blk_cut(cblk(p, -side[way]), k)]
-                wire.take(("g", h, way, p, 0, k), spot, any_dev)
+                d = -side[way]
+                wire.take(("g", h, way, p, 0, k), gh[h].at[blk_cut(cblk(p, d), k)], any_dev)
                 if way == way_of(k):
-                    wire.push(("g", h, way, p, 1, k), spot, spot, col_to[way])
+                    g_pass(h, p, d, k, way, 1)
+                if k in kind_a:
+                    g_pass(h, p, d, k, "Y", d)
 
     def g_far(h, k):
-        for p in (0, 1):
+        for p in (0,) if k in kind_a else (0, 1):
             wire.take(("g", h, way_of(k), p, 1, k), gh[h].at[blk_cut(cblk(p, 2), k)], any_dev)
-
-    r_in = {"R": in_r, "L": in_l}
+            if k in kind_a:
+                g_pass(h, p, 2, k, "Y", 2)
+
+    def g_last(h):
+        for k in kind_a:
+            for d in (1, -1, 2):
+                wire.take(("g", h, "Y", 0, d, k), gh[h].at[blk_cut(cblk(1, d), k)], any_dev)
+
     rel = lambda p, d: p * RING + d % RING
     arrived = set()
 
-    def r_start(h):
+    def sib_push(h):
         for d in (2, 1, -1, 0):
             for p in (1, 0):
                 there = pl.ds(rblk(p, d, 1) * nbd, nbd)
                 wire.push(("s", h, rel(p, d)), back.at[h, there], sib_in.at[h, rel(p, d)], row_to["S"])
 
-    def both(h, p, d, k):
+    def r_base(h, p, d, k):
         key = ("s", h, rel(p, d))
         if key not in arrived:
             arrived.add(key)
             wire.take(key, sib_in.at[h, rel(p, d)], any_dev)
         return f(back[h, blk_cut(rblk(p, d), k)]) + f(sib_in[h, rel(p, d), cut(k)])
 
-    def r_far(h, k):
-        for p in (1, 0):
-            o_out[h, p, cut(k)] = both(h, p, 2, k).astype(bf16)
-            wire.push(("r", h, "opp", p, k), o_out.at[h, p, cut(k)], o_in.at[h, p, cut(k)], row_to[way_of(k)])
-
-    def r_near(h, k):
-        w = other[way_of(k)]
-        for p in (1, 0):
-            d_out[h, p, cut(k)] = both(h, p, side[w], k).astype(bf16)
-            wire.push(("r", h, w, p, k), d_out.at[h, p, cut(k)], r_in[w].at[h, p, cut(k)], row_to[w])
-
-    def r_ring(h, k):
-        w = way_of(k)
-        for p in (1, 0):
-            base = both(h, p, side[w], k)
-            wire.take(("r", h, "opp", p, k), o_in.at[h, p, cut(k)], any_dev)
-            t_out[h, p, cut(k)] = (base + f(o_in[h, p, cut(k)])).astype(bf16)
-            wire.push(("r", h, w, p, k), t_out.at[h, p, cut(k)], r_in[w].at[h, p, cut(k)], row_to[w])
-
-    def r_sum(h, p, k):
-        base = both(h, p, 0, k)
-        for w in "RL":
-            wire.take(("r", h, w, p, k), r_in[w].at[h, p, cut(k)], any_dev)
-        return base + f(in_r[h, p, cut(k)]) + f(in_l[h, p, cut(k)])
-
-    def r_pair(h, k):
-        s_out[h, cut(k)] = r_sum(h, 1, k).astype(bf16)
-        wire.push(("r", h, "y", k), s_out.at[h, cut(k)], y_in.at[h, cut(k)], row_to["Y"])
+    rs = Sums("r", row_to, r_base, None, r_bufs)
 
     def r_end(h, k):
-        total = r_sum(h, 0, k)
-        wire.take(("r", h, "y", k), y_in.at[h, cut(k)], any_dev)
-        total = (total + f(y_in[h, cut(k)])).astype(bf16)
-        gfeat[pl.ds(k * rows, rows), h * LANES:(h + 1) * LANES] = total.reshape(rows, LANES)
-
-    def pipeline(stages, n):
-        return [step_of(stage, k) for tick in range(n + len(stages) - 1)
-                for s, stage in enumerate(stages) for k in [tick - s] if 0 <= k < n]
-
-    def r_steps(h):
-        steps = [step_of(r_far, h, k) for k in chunks] + [step_of(r_near, h, k) for k in chunks]
-        steps += [step_of(r_ring, h, k) for k in chunks]
-        return steps + pipeline([lambda k: r_pair(h, k), lambda k: r_end(h, k)], nk)
+        gfeat[pl.ds(k * rows, rows), h * LANES:(h + 1) * LANES] = rs.end(h, k).reshape(rows, LANES)
 
     half = term.shape[0] // 2
     eighth = half // (2 * RING)
@@ -488,54 +529,126 @@
         wire.take("w4", w_full.at[hd(1 - core)], any_dev)
         gw[...] = w_full[...]
 
+    loads[0].wait()
+    for h in (0, 1):
+        src[h][pl.ds(rblk(0, 0) * nbd, nbd)] = feat[:, h * LANES:(h + 1) * LANES].reshape(nbd, BLOCK, LANES)
+    met()
     own0, steps0 = gather(0)
     own1, steps1 = gather(1)
     own0()
-    load.wait()
+    loads[1].wait()
     for s in range(0, tiles, 16):
         m[s:s + 16] = vals[s:s + 16].reshape((16,) + m.shape[1:])
     m[tiles:] = jnp.zeros((1,) + m.shape[1:], bf16)
     for i, step in enumerate(steps0):
         step()
-        if i == 5:
+        if i == 8:
             own1()
-    weave(products(0, lhs_fwd, rhs_fwd, 2, gf, 7), steps1[:-1])
+
+    def each(fn, h, ks):
+        for k in ks:
+            fn(h, k)
+
+    def run(steps):
+        for step in steps:
+            step()
+
+    work = products(0, lhs_fwd, rhs_fwd, 2, gf, 3)
+    work[0]()
+    run(steps1[:5])
+    work[1]()
+    run(steps1[5:9])
+    work[2]()
     settle(part, 0, 3, gf, nr)
-    c_start(0)
-    steps1[-1]()
-    c_steps = [step_of(c_ring, 0, k) for k in chunks]
-    c_steps += pipeline([lambda k: c_pair(0, k), lambda k: c_end(0, k)], nk)
-    weave(products(1, lhs_fwd, rhs_fwd, 2, gf, 7), c_steps)
+    run(cs.begin(0))
+    run(steps1[9:])
+    work = products(1, lhs_fwd, rhs_fwd, 2, gf, 3)
+    work[0]()
+    each(cs.ring, 0, kind_b)
+    run(cs.second(0))
+    work[1]()
+    work[2]()
     settle(part, 1, 3, gf, nr)
-    c_start(1)
+    run(cs.begin(1))
+    each(cs.ring, 0, kind_a)
+    each(cs.pair, 0, kind_b)
+    for load in loads[2:]:
+        load.wait()
+    each(cs.ring, 1, kind_b)
+    run(cs.second(1))
+    each(c_end, 0, chunks)
+    each(cs.ring, 1, kind_a)
+    each(cs.pair, 1, kind_b)
     for k in chunks:
-        c_ring(1, k)
-    def finish(k):
         c_end(1, k)
         dense(k)
-
-    for step in pipeline([lambda k: c_pair(1, k), finish, lambda k: g_pair(0, k)], nk):
-        step()
-    for k in chunks:
-        g_push(1, k)
     w0()
-    for step in pipeline([lambda k: g_ring(0, k), lambda k: g_far(0, k)], nk):
-        step()
-    g_steps = [step_of(g_pair, 1, k) for k in chunks] + [w1] + [step_of(g_ring, 1, k) for k in chunks] + [w2]
-    g_steps += [step_of(g_far, 1, k) for k in chunks] + [w3]
-    weave(products(0, lhs_bwd, rhs_bwd, 6, gb, 9), g_steps)
+    each(g_pair, 0, kind_b)
+    each(g_ring, 0, chunks[:2])
+    each(g_far, 0, kind_a)
+    each(g_ring, 0, chunks[2:])
+    each(g_push, 1, chunks)
+    each(g_pair, 0, kind_a)
+    each(g_far, 0, kind_b)
+    g_last(0)
+    work = products(0, lhs_bwd, rhs_bwd, 6, gb, 3)
+    work[0]()
+    w1()
+    each(g_pair, 1, kind_b)
+    each(g_ring, 1, kind_a)
+    work[1]()
+    each(g_far, 1, kind_a)
+    each(g_ring, 1, kind_b)
+    w2()
+    work[2]()
     settle(back, 0, 7, gb, nc)
-    r_start(0)
-    weave(products(1, lhs_bwd, rhs_bwd, 6, gb, 9), r_steps(0) + [w4])
+    sib_push(0)
+    each(g_pair, 1, kind_a)
+    each(g_far, 1, kind_b)
+    g_last(1)
+    run(rs.begin(0))
+    work = products(1, lhs_bwd, rhs_bwd, 6, gb, 3)
+    work[0]()
+    run(rs.second(0))
+    w3()
+    work[1]()
+    each(rs.ring, 0, kind_b)
+    work[2]()
     settle(back, 1, 7, gb, nc)
-    r_start(1)
-    for step in r_steps(1):
-        step()
+    sib_push(1)
+    each(rs.ring, 0, kind_a)
+    each(rs.pair, 0, kind_b)
+    run(rs.begin(1))
+    w4()
+    each(rs.ring, 1, kind_b)
+    run(rs.second(1))
+    each(r_end, 0, chunks)
+    each(rs.ring, 1, kind_a)
+    each(rs.pair, 1, kind_b)
+    each(r_end, 1, chunks)
     w5()
     wire.drain()
 
 
-def layer(lists, features, values, weight, grad_out, nr, nc):
+def place_kernel(*refs):
+    count = len(refs) // 2
+    for i in range(count):
+        refs[count + i][...] = refs[i][...]
+
+
+def place(*arrays):
+    n = len(arrays)
+    return pl.pallas_call(
+        place_kernel,
+        out_shape=[jax.ShapeDtypeStruct(a.shape, a.dtype) for a in arrays],
+        in_specs=[pl.BlockSpec(memory_space=VM)] * n,
+        out_specs=[pl.BlockSpec(memory_space=VM)] * n,
+        compiler_params=pltpu.CompilerParams(vmem_limit_bytes=60 << 20),
+        name="place",
+    )(*arrays)
+
+
+def layer(lists, features, weight, grad_out, values, nr, nc):
     rows, width = features.shape
     tiles = values.shape[0]
     nbd = rows // BLOCK
@@ -545,36 +658,36 @@
     wf = lambda *lead: pltpu.VMEM(lead + (wrows,), f32)
     eighth = wrows // (4 * RING)
     two = 2
+    two_ring = piece(two, 2, nbd)
+    sums = [piece(two, RING, nbd // 2)] * 2 + [two_ring] * 6 + [piece(two, nbd)] * 2
     scratch = [
+        pltpu.VMEM(features.shape, bf16), pltpu.VMEM(weight.shape, bf16), pltpu.VMEM(grad_out.shape, bf16),
         pltpu.VMEM(values.shape, bf16), pltpu.VMEM((tiles + 1, BLOCK // 2, 2 * BLOCK), bf16),
         piece(nc), piece(nc), piece(gmax + 1), piece(two, nr),
-        piece(two, 2, nbd), piece(two, 2, nbd), piece(two, 2, nbd), piece(two, 2, nbd),
-        piece(two, nbd), piece(two, nbd), piece(two, nbd), piece(two, nbd), piece(nr), piece(nr), piece(two, nc),
-        piece(two, 2 * RING, nbd), piece(two, 2, nbd), piece(two, 2, nbd), piece(two, 2, nbd), piece(two, 2, nbd),
-        piece(two, 2, nbd), piece(two, 2, nbd), piece(two, nbd), piece(two, nbd),
+        sums, piece(two, nbd), piece(two, nbd), piece(nr), piece(nr), piece(two, nc),
+        piece(two, 2 * RING, nbd), sums,
         wf(wrows), wf(wrows // 2), wf(wrows // 2), wf(2 * RING - 1, eighth), wf(2 * RING, eighth), wf(eighth), wf(wrows),
-        pltpu.SemaphoreType.DMA((400,)), pltpu.SemaphoreType.DMA((400,)), pltpu.SemaphoreType.DMA,
+        pltpu.SemaphoreType.DMA((400,)), pltpu.SemaphoreType.DMA((400,)), pltpu.SemaphoreType.DMA((4,)),
     ]
     return pl.pallas_call(
         layer_kernel,
         out_shape=[jax.ShapeDtypeStruct((rows, width), bf16), jax.ShapeDtypeStruct((rows, width), bf16),
                    jax.ShapeDtypeStruct((wrows, width), f32)],
-        in_specs=[pl.BlockSpec(memory_space=pltpu.SMEM), pl.BlockSpec(memory_space=VM), pl.BlockSpec(memory_space=pl.ANY),
-                  pl.BlockSpec(memory_space=VM), pl.BlockSpec(memory_space=VM)],
+        in_specs=[pl.BlockSpec(memory_space=pltpu.SMEM)] + [pl.BlockSpec(memory_space=pl.ANY)] * 4,
         out_specs=[pl.BlockSpec(memory_space=VM)] * 3,
         scratch_shapes=scratch,
-        compiler_params=pltpu.CompilerParams(collective_id=1, has_side_effects=True, vmem_limit_bytes=60 << 20),
+        compiler_params=pltpu.CompilerParams(collective_id=1, has_side_effects=True, vmem_limit_bytes=58 << 20),
         name="layer",
-    )(lists, features, values, weight, grad_out)
+    )(lists, features, weight, grad_out, values)
 
 
 def per_device(features, weight, grad_out, tile_rows, tile_cols, tile_values, tile_counts):
     nodes_dev = features.shape[0]
     nr = nodes_dev * lax.axis_size("col") // BLOCK
     nc = nodes_dev * lax.axis_size("row") // BLOCK
+    values = tile_values.reshape(tile_values.shape[2:])
     lists = make_lists(tile_rows, tile_cols, tile_counts, nr, nc)
-    values = tile_values.reshape(tile_values.shape[2:])
-    return tuple(layer(lists, features, values, weight, grad_out, nr, nc))
+    return tuple(place(*layer(lists, features, weight, grad_out, values, nr, nc)))
 
 
 def solution(mesh):

time: 175 us -> 142 us (0.81)
  Pallas kernels: 165 us -> 140 us
  local copies, waits for them, and re-layouts: 7.18 us -> 0 us
    pallas_call x1, Pallas kernels: 163 us -> 134 us  [layer(): pl.pallas_call(layer_kernel, out_shape=[jax.ShapeDtypeStruct((rows, width...]
    unnamed x9 -> x0, local copies, waits for them, and re-layouts: 7.18 us -> none
    pallas_call x1 -> x2, Pallas kernels: 2.05 us -> 5.59 us  [the longest x1 3.41 us: make_lists(): pl.pallas_call(functools.partial(lists_kernel, tiles, nr, nc), out_shape=...]
where the time goes in v5:
time: 142 us; the launch traced here: 141 us
  Pallas kernels  140 us (99%)
    pallas_call x1, Pallas kernels, layer(): pl.pallas_call(layer_kernel, out_shape=[jax.ShapeDtypeStruct((rows, width...  134 us
    pallas_call x1, Pallas kernels, make_lists(): pl.pallas_call(functools.partial(lists_kernel, tiles, nr, nc), out_shape=...  3.41 us

profile of v5, /device:TPU:0, one launch (start us, length us, event | category | flops | bytes accessed | tf_op | source)
XLA Modules:
  0.0 141.2 jit_solution(14819093632269905439)
XLA Ops:
  1.3 3.4 %lists.1 = s32[8,1280]{1,0:T(8,128)} custom-call(s32[1,1,608]{2,1,0:T(1,128)} %rows_in.1, s32[1,1,608]{2,1,0:T(1,128)} %cols_in.1, s32[1,1]{1,0:T(1,128)S(6)} %copy.10.count_ref), custom_call_target="tpu_custom_call" | custom-call | tf_op jit(solution)/shard_map/lists/pallas_call | solution.py:81
  4.7 134.3 %layer.1 = (bf16[768,256]{1,0:T(8,128)(2,1)}, bf16[768,256]{1,0:T(8,128)(2,1)}, f32[256,256]{1,0:T(8,128)}) custom-call(s32[8,1280]{1,0:T(8,128)} %lists.1, bf16[768,256]{1,0:T(8,128)(2,1)} %feat_in.1, bf16[256,256]{1,0:T(8,128)(2,1)} %weight_in.1, bf16[768,256]{1,0:T(8,128)(2,1)} %gout_in.1, bf16[608,4096]{1,0:T(8,128)(2,1)} %bitcast.1), custom_call_target="tpu_custom_call" | custom-call | tf_op jit(solution)/shard_map/layer/pallas_call | solution.py:672
  139.0 2.2 %place.1 = (bf16[768,256]{1,0:T(8,128)(2,1)}, bf16[768,256]{1,0:T(8,128)(2,1)}, f32[256,256]{1,0:T(8,128)}) custom-call(bf16[768,256]{1,0:T(8,128)(2,1)} %get-tuple-element.6.refs_0_, bf16[768,256]{1,0:T(8,128)(2,1)} %get-tuple-element.7.refs_1_, f32[256,256]{1,0:T(8,128)} %get-tuple-element.8.refs_2_), custom_call_target="tpu_custom_call" | custom-call | tf_op jit(solution)/shard_map/place/pallas_call | solution.py:641

commit v6 on v5

--- a/solution.py
+++ b/solution.py
@@ -186,66 +186,72 @@
     side = {"R": 1, "L": -1}
     other = {"R": "L", "L": "R"}
 
-    cb = nbd // 2
+    nk = 6
+    ck = nbd // nk
+    chunks = range(nk)
+    kind_a, kind_b = chunks[:2], chunks[2:]
+    way_of = lambda k: "R" if k % 2 == 0 else "L"
+    cut = lambda k: pl.ds(k * ck, ck)
+    blk_cut = lambda b, k: pl.ds(b * nbd + k * ck, ck)
 
     def gather(h):
-        def slot(p, d, s, k, part_):
-            size = cb if part_ is None else cb // 2
-            at = rblk(p, d, s) * nbd + k * cb + (0 if part_ is None else part_ * size)
-            return src[h].at[pl.ds(at, size)]
-
-        def push(way, p, d, k, part_=None):
-            spot = slot(p, d, 0, k, part_)
-            wire.push(("f", h, way, p, d % RING, k, part_), spot, spot, row_to[way])
-
-        def take(way, p, d, k, part_=None):
-            key = ("f", h, way, p, d % RING, k, part_)
+        def slot(p, d, s, k):
+            return src[h].at[blk_cut(rblk(p, d, s), k)]
+
+        def push(way, p, d, k):
+            spot = slot(p, d, 0, k)
+            wire.push(("f", h, way, p, d % RING, k), spot, spot, row_to[way])
+
+        def take(way, p, d, k):
+            key = ("f", h, way, p, d % RING, k)
             if way == "S":
-                wire.take(key, slot(p, d, 1, k, part_), any_dev)
+                wire.take(key, slot(p, d, 1, k), any_dev)
                 return
             q, e = {"R": (p, d - 1), "L": (p, d + 1), "Y": (1 - p, d)}[way]
-            wire.take(key, slot(q, e, 0, k, part_), any_dev)
+            wire.take(key, slot(q, e, 0, k), any_dev)
             if way == "Y":
-                if k == 1:
+                if k in kind_b:
                     push("R", q, e, k)
                     push("L", q, e, k)
             else:
-                if abs(e) == 1:
-                    push(way, q, e, k, 0 if way == "R" else 1)
-                if k == 0:
-                    push("Y", q, e, k, part_)
-            push("S", q, e, k, part_)
+                if abs(e) == 1 and way == way_of(k):
+                    push(way, q, e, k)
+                if k in kind_a:
+                    push("Y", q, e, k)
+            push("S", q, e, k)
 
         def own():
-            push("Y", 0, 0, 1)
-            for k in (0, 1):
-                for way in "RL":
-                    push(way, 0, 0, k)
-            for k in (0, 1):
+            for k in kind_b:
+                push("Y", 0, 0, k)
+            for k in chunks:
+                push("R", 0, 0, k)
+                push("L", 0, 0, k)
+            for k in chunks:
                 push("S", 0, 0, k)
 
         def own_late():
-            push("Y", 0, 0, 0)
-
-        order = [("Y", 0, 0, 1), ("R", 0, 0, 0), ("L", 0, 0, 0), ("R", 0, 0, 1), ("L", 0, 0, 1),
-                 ("R", 0, -1, 0, 0), ("L", 0, 1, 0, 1), ("R", 1, 0, 1), ("L", 1, 0, 1),
-                 ("Y", 0, 0, 0), ("Y", 0, -1, 0), ("Y", 0, 1, 0)]
-        order += [("R", p, -1, 1, 0) if way == "R" else ("L", p, 1, 1, 1) for p in (0, 1) for way in "RL"]
-        order += [("Y", 0, -2, 0, 0), ("Y", 0, 2, 0, 1)]
-        steps = [step_of(take, *o) for o in order]
-        first = steps[2]
-
-        def third():
-            first()
-            own_late()
-
-        steps[2] = third
+            for k in kind_a:
+                push("Y", 0, 0, k)
+
+        def far(p, k):
+            take(*(("R", p, -1, k) if way_of(k) == "R" else ("L", p, 1, k)))
 
         def close():
             for key in [key for key in wire.ids if key[:3] == ("f", h, "S")]:
                 take("S", *key[3:])
 
-        return own, steps + [close]
+        near = lambda p, k: [step_of(take, way, p, 0, k) for way in "RL"]
+        early = [step_of(take, "Y", 0, 0, k) for k in kind_b]
+        for i, k in enumerate(kind_a):
+            early[3 * i + 1:3 * i + 1] = near(0, k)
+        early.append(own_late)
+        middle = [x for k in kind_b for x in near(0, k)] + [step_of(far, 0, k) for k in kind_a]
+        late = [x for k in kind_b for x in near(1, k)]
+        rest = [step_of(take, "Y", 0, 0, k) for k in kind_a]
+        rest += [step_of(take, "Y", 0, d, k) for k in kind_a for d in (-1, 1)]
+        rest += [step_of(far, 0, k) for k in kind_b] + [step_of(far, 1, k) for k in kind_b]
+        rest += [step_of(take, "Y", 0, 2, k) for k in kind_a] + [close]
+        return own, early, middle, late, rest
 
     low = lax.broadcasted_iota(i32, (BLOCK // 2, 2 * BLOCK), 1) < BLOCK
 
@@ -297,15 +303,6 @@
 
         lax.fori_loop(0, blocks // 8, body, 0)
 
-    nk = 4
-    ck = nbd // nk
-    chunks = range(nk)
-    kind_a, kind_b = chunks[:1], chunks[1:]
-    ca = len(kind_a) * ck
-    way_of = lambda k: "R" if k % 2 == 0 else "L"
-    cut = lambda k: pl.ds(k * ck, ck)
-    blk_cut = lambda b, k: pl.ds(b * nbd + k * ck, ck)
-
     class Sums:
         def __init__(self, tag, to, base, ref, bufs):
             self.tag, self.to, self.base, self.ref = tag, to, base, ref
@@ -314,47 +311,53 @@
             self.inn = {"R": self.r_in, "L": self.l_in}
             self.got = set()
 
+        def kinds(self, h):
+            n = 2 - h
+            return chunks[:n], chunks[n:]
+
         def ya(self, h, d):
+            size = len(self.kinds(h)[0]) * ck
             if self.ref is not None:
-                spot = self.ref(h, 1, d, None)
+                spot = self.ref(h, 1, d, 0, size)
             else:
-                for k in kind_a:
+                for k in self.kinds(h)[0]:
                     self.ya_out[h, d % RING, cut(k)] = self.base(h, 1, d, k).astype(bf16)
-                spot = self.ya_out.at[h, d % RING, pl.ds(0, ca)]
-            wire.push((self.tag, h, "ya", d % RING), spot, self.ya_in.at[h, d % RING, pl.ds(0, ca)], self.to["Y"])
+                spot = self.ya_out.at[h, d % RING, pl.ds(0, size)]
+            wire.push((self.tag, h, "ya", d % RING), spot, self.ya_in.at[h, d % RING, pl.ds(0, size)], self.to["Y"])
 
         def term(self, h, p, d, k):
+            kind_a, kind_b = self.kinds(h)
             if k in kind_b:
                 return self.base(h, p, d, k)
             key = (self.tag, h, "ya", d % RING)
             if key not in self.got:
                 self.got.add(key)
-                wire.take(key, self.ya_in.at[h, d % RING, pl.ds(0, ca)], any_dev)
+                wire.take(key, self.ya_in.at[h, d % RING, pl.ds(0, len(kind_a) * ck)], any_dev)
             return self.base(h, 0, d, k) + f(self.ya_in[h, d % RING, cut(k)])
 
-        def ps(self, k):
-            return (0,) if k in kind_a else (1, 0)
+        def ps(self, h, k):
+            return (0,) if k in self.kinds(h)[0] else (1, 0)
 
         def _out(self, h, p, d, k, buf):
-            if self.ref is not None and k in kind_b:
+            if self.ref is not None and k in self.kinds(h)[1]:
                 return self.ref(h, p, d, k)
             buf[h, p, cut(k)] = self.term(h, p, d, k).astype(bf16)
             return buf.at[h, p, cut(k)]
 
         def far(self, h, k):
-            for p in self.ps(k):
+            for p in self.ps(h, k):
                 wire.push((self.tag, h, "opp", p, k), self._out(h, p, 2, k, self.o_out), self.o_in.at[h, p, cut(k)],
                           self.to[way_of(k)])
 
         def near(self, h, k):
             w = other[way_of(k)]
-            for p in self.ps(k):
+            for p in self.ps(h, k):
                 wire.push((self.tag, h, w, p, k), self._out(h, p, side[w], k, self.n_out), self.inn[w].at[h, p, cut(k)],
                           self.to[w])
 
         def ring(self, h, k):
             w = way_of(k)
-            for p in self.ps(k):
+            for p in self.ps(h, k):
                 own = self.term(h, p, side[w], k)
                 wire.take((self.tag, h, "opp", p, k), self.o_in.at[h, p, cut(k)], any_dev)
                 self.t_out[h, p, cut(k)] = (own + f(self.o_in[h, p, cut(k)])).astype(bf16)
@@ -367,30 +370,32 @@
             return own + f(self.r_in[h, p, cut(k)]) + f(self.l_in[h, p, cut(k)])
 
         def pair(self, h, k):
-            if k in kind_b:
+            if k in self.kinds(h)[1]:
                 self.s_out[h, cut(k)] = self.total(h, 1, k).astype(bf16)
                 wire.push((self.tag, h, "y", k), self.s_out.at[h, cut(k)], self.y_in.at[h, cut(k)], self.to["Y"])
 
         def end(self, h, k):
             value = self.total(h, 0, k)
-            if k in kind_b:
+            if k in self.kinds(h)[1]:
                 wire.take((self.tag, h, "y", k), self.y_in.at[h, cut(k)], any_dev)
                 value = value + f(self.y_in[h, cut(k)])
             return value.astype(bf16)
 
         def begin(self, h):
-            return ([step_of(self.ya, h, 2)] + [step_of(self.far, h, k) for k in kind_b]
-                    + [step_of(self.ya, h, d) for d in (1, -1)] + [step_of(self.near, h, k) for k in kind_b]
-                    + [step_of(self.ya, h, 0)])
+            kind_b = self.kinds(h)[1]
+            steps = [step_of(self.ya, h, d) for d in (2, 1, -1)] + [step_of(self.far, h, k) for k in kind_b]
+            steps += [step_of(self.ya, h, 0)]
+            return steps, [step_of(self.near, h, k) for k in kind_b]
 
         def second(self, h):
+            kind_a = self.kinds(h)[0]
             return [step_of(self.far, h, k) for k in kind_a] + [step_of(self.near, h, k) for k in kind_a]
 
     def c_base(h, p, d, k):
         return f(part[h, blk_cut(cblk(p, d), k)])
 
-    def c_ref(h, p, d, k):
-        return part.at[h, pl.ds(cblk(p, d) * nbd, ca) if k is None else blk_cut(cblk(p, d), k)]
+    def c_ref(h, p, d, k, size=ck):
+        return part.at[h, pl.ds(cblk(p, d) * nbd + k * ck, size)]
 
     cs = Sums("c", col_to, c_base, c_ref, c_bufs)
 
@@ -404,9 +409,10 @@
     node = i0 - inside + jnp.where(inside < BLOCK // 2, 2 * inside, 2 * inside - (BLOCK - 1))
     order = (node == i1).astype(f32).astype(bf16)
 
-    def g_push(h, k):
-        for way in "YRL":
-            wire.push(("g", h, way, 0, 0, k), gl.at[h, cut(k)], gh[h].at[blk_cut(cblk(0, 0), k)], col_to[way])
+    def g_push(h, ks, ways):
+        for k in ks:
+            for way in ways:
+                wire.push(("g", h, way, 0, 0, k), gl.at[h, cut(k)], gh[h].at[blk_cut(cblk(0, 0), k)], col_to[way])
 
     def g_pass(h, p, d, k, way, hop):
         spot = gh[h].at[blk_cut(cblk(p, d), k)]
@@ -424,7 +430,7 @@
         for h in (0, 1):
             mine = local[:, h * LANES:(h + 1) * LANES].reshape(ck, BLOCK, LANES)
             gl[h, cut(k)] = mine
-        g_push(0, k)
+        g_push(0, (k,), "YRL")
         for h in (0, 1):
             gh[h][blk_cut(cblk(0, 0), k)] = gl[h, cut(k)]
         out[at] = lax.dot_general(order, act.astype(bf16), (((0,), (0,)), ((), ())),
@@ -533,18 +539,13 @@
     for h in (0, 1):
         src[h][pl.ds(rblk(0, 0) * nbd, nbd)] = feat[:, h * LANES:(h + 1) * LANES].reshape(nbd, BLOCK, LANES)
     met()
-    own0, steps0 = gather(0)
-    own1, steps1 = gather(1)
+    own0, *steps0 = gather(0)
+    own1, *steps1 = gather(1)
     own0()
     loads[1].wait()
     for s in range(0, tiles, 16):
         m[s:s + 16] = vals[s:s + 16].reshape((16,) + m.shape[1:])
     m[tiles:] = jnp.zeros((1,) + m.shape[1:], bf16)
-    for i, step in enumerate(steps0):
-        step()
-        if i == 8:
-            own1()
-
     def each(fn, h, ks):
         for k in ks:
             fn(h, k)
@@ -553,78 +554,91 @@
         for step in steps:
             step()
 
-    work = products(0, lhs_fwd, rhs_fwd, 2, gf, 3)
-    work[0]()
-    run(steps1[:5])
-    work[1]()
-    run(steps1[5:9])
-    work[2]()
+    run(steps0[0] + steps0[1] + steps0[2])
+    own1()
+    run(steps0[3])
+    early, middle, late, rest = steps1
+    some_a, some_b = cs.kinds(1)
+    work = products(0, lhs_fwd, rhs_fwd, 2, gf, 7)
+    turns = [early, middle[:4], middle[4:8], late[:4], late[4:], middle[8:], []]
+    for piece, steps in zip(work, turns):
+        piece()
+        run(steps)
     settle(part, 0, 3, gf, nr)
-    run(cs.begin(0))
-    run(steps1[9:])
+    run(sum(cs.begin(0), []))
+    run(rest)
     work = products(1, lhs_fwd, rhs_fwd, 2, gf, 3)
     work[0]()
-    each(cs.ring, 0, kind_b)
+    each(cs.ring, 0, cs.kinds(0)[1])
     run(cs.second(0))
     work[1]()
     work[2]()
+    each(cs.ring, 0, cs.kinds(0)[0])
     settle(part, 1, 3, gf, nr)
-    run(cs.begin(1))
-    each(cs.ring, 0, kind_a)
-    each(cs.pair, 0, kind_b)
+    run(sum(cs.begin(1), []))
+    each(cs.pair, 0, cs.kinds(0)[1])
     for load in loads[2:]:
         load.wait()
-    each(cs.ring, 1, kind_b)
+    each(cs.ring, 1, some_b[:1])
     run(cs.second(1))
+    each(cs.ring, 1, some_b[1:3])
     each(c_end, 0, chunks)
-    each(cs.ring, 1, kind_a)
-    each(cs.pair, 1, kind_b)
+    each(cs.ring, 1, some_a)
+    each(cs.ring, 1, some_b[3:])
+    each(cs.pair, 1, cs.kinds(1)[1])
     for k in chunks:
         c_end(1, k)
         dense(k)
     w0()
+    each(g_ring, 0, kind_a)
     each(g_pair, 0, kind_b)
-    each(g_ring, 0, chunks[:2])
+    each(g_ring, 0, kind_b[:2])
     each(g_far, 0, kind_a)
-    each(g_ring, 0, chunks[2:])
-    each(g_push, 1, chunks)
+    each(g_ring, 0, kind_b[2:])
+    g_push(1, kind_b, "Y")
+    g_push(1, chunks, "RL")
+    g_push(1, kind_a, "Y")
     each(g_pair, 0, kind_a)
     each(g_far, 0, kind_b)
     g_last(0)
-    work = products(0, lhs_bwd, rhs_bwd, 6, gb, 3)
+    work = products(0, lhs_bwd, rhs_bwd, 6, gb, 5)
     work[0]()
+    each(g_ring, 1, kind_a)
+    each(g_pair, 1, kind_b)
     w1()
-    each(g_pair, 1, kind_b)
-    each(g_ring, 1, kind_a)
     work[1]()
+    each(g_ring, 1, kind_b[:2])
+    work[2]()
     each(g_far, 1, kind_a)
-    each(g_ring, 1, kind_b)
+    each(g_ring, 1, kind_b[2:])
+    work[3]()
     w2()
-    work[2]()
+    work[4]()
     settle(back, 0, 7, gb, nc)
     sib_push(0)
     each(g_pair, 1, kind_a)
     each(g_far, 1, kind_b)
     g_last(1)
-    run(rs.begin(0))
+    run(sum(rs.begin(0), []))
     work = products(1, lhs_bwd, rhs_bwd, 6, gb, 3)
     work[0]()
-    run(rs.second(0))
     w3()
     work[1]()
-    each(rs.ring, 0, kind_b)
+    run(rs.second(0))
+    each(rs.ring, 0, rs.kinds(0)[1])
     work[2]()
+    each(rs.ring, 0, rs.kinds(0)[0])
     settle(back, 1, 7, gb, nc)
     sib_push(1)
-    each(rs.ring, 0, kind_a)
-    each(rs.pair, 0, kind_b)
-    run(rs.begin(1))
+    some, more = rs.begin(1)
+    run(some + rs.second(1) + more)
+    each(rs.pair, 0, rs.kinds(0)[1])
     w4()
-    each(rs.ring, 1, kind_b)
-    run(rs.second(1))
+    each(rs.ring, 1, some_b[:3])
+    each(rs.ring, 1, some_a)
+    each(rs.ring, 1, some_b[3:])
     each(r_end, 0, chunks)
-    each(rs.ring, 1, kind_a)
-    each(rs.pair, 1, kind_b)
+    each(rs.pair, 1, rs.kinds(1)[1])
     each(r_end, 1, chunks)
     w5()
     wire.drain()
@@ -659,7 +673,7 @@
     eighth = wrows // (4 * RING)
     two = 2
     two_ring = piece(two, 2, nbd)
-    sums = [piece(two, RING, nbd // 2)] * 2 + [two_ring] * 6 + [piece(two, nbd)] * 2
+    sums = [piece(two, RING, nbd // 3)] * 2 + [two_ring] * 6 + [piece(two, nbd)] * 2
     scratch = [
         pltpu.VMEM(features.shape, bf16), pltpu.VMEM(weight.shape, bf16), pltpu.VMEM(grad_out.shape, bf16),
         pltpu.VMEM(values.shape, bf16), pltpu.VMEM((tiles + 1, BLOCK // 2, 2 * BLOCK), bf16),
@@ -667,7 +681,7 @@
         sums, piece(two, nbd), piece(two, nbd), piece(nr), piece(nr), piece(two, nc),
         piece(two, 2 * RING, nbd), sums,
         wf(wrows), wf(wrows // 2), wf(wrows // 2), wf(2 * RING - 1, eighth), wf(2 * RING, eighth), wf(eighth), wf(wrows),
-        pltpu.SemaphoreType.DMA((400,)), pltpu.SemaphoreType.DMA((400,)), pltpu.SemaphoreType.DMA((4,)),
+        pltpu.SemaphoreType.DMA((512,)), pltpu.SemaphoreType.DMA((512,)), pltpu.SemaphoreType.DMA((4,)),
     ]
     return pl.pallas_call(
         layer_kernel,

time: 142 us -> 139 us (0.979)
  Pallas kernels: 140 us -> 137 us
    pallas_call x1, Pallas kernels: 134 us -> 132 us  [layer(): pl.pallas_call(layer_kernel, out_shape=[jax.ShapeDtypeStruct((rows, width...]
where the time goes in v6:
time: 139 us; the launch traced here: 138 us
  Pallas kernels  137 us (99%)
    pallas_call x1, Pallas kernels, layer(): pl.pallas_call(layer_kernel, out_shape=[jax.ShapeDtypeStruct((rows, width...  132 us
    pallas_call x1, Pallas kernels, make_lists(): pl.pallas_call(functools.partial(lists_kernel, tiles, nr, nc), out_shape=...  3.41 us

profile of v6, /device:TPU:0, one launch (start us, length us, event | category | flops | bytes accessed | tf_op | source)
XLA Modules:
  0.0 138.5 jit_solution(3488990679008920676)
XLA Ops:
  1.3 3.4 %lists.1 = s32[8,1280]{1,0:T(8,128)} custom-call(s32[1,1,608]{2,1,0:T(1,128)} %rows_in.1, s32[1,1,608]{2,1,0:T(1,128)} %cols_in.1, s32[1,1]{1,0:T(1,128)S(6)} %copy.10.count_ref), custom_call_target="tpu_custom_call" | custom-call | tf_op jit(solution)/shard_map/lists/pallas_call | solution.py:81
  4.7 131.6 %layer.1 = (bf16[768,256]{1,0:T(8,128)(2,1)}, bf16[768,256]{1,0:T(8,128)(2,1)}, f32[256,256]{1,0:T(8,128)}) custom-call(s32[8,1280]{1,0:T(8,128)} %lists.1, bf16[768,256]{1,0:T(8,128)(2,1)} %feat_in.1, bf16[256,256]{1,0:T(8,128)(2,1)} %weight_in.1, bf16[768,256]{1,0:T(8,128)(2,1)} %gout_in.1, bf16[608,4096]{1,0:T(8,128)(2,1)} %bitcast.1), custom_call_target="tpu_custom_call" | custom-call | tf_op jit(solution)/shard_map/layer/pallas_call | solution.py:686
  136.3 2.2 %place.1 = (bf16[768,256]{1,0:T(8,128)(2,1)}, bf16[768,256]{1,0:T(8,128)(2,1)}, f32[256,256]{1,0:T(8,128)}) custom-call(bf16[768,256]{1,0:T(8,128)(2,1)} %get-tuple-element.6.refs_0_, bf16[768,256]{1,0:T(8,128)(2,1)} %get-tuple-element.7.refs_1_, f32[256,256]{1,0:T(8,128)} %get-tuple-element.8.refs_2_), custom_call_target="tpu_custom_call" | custom-call | tf_op jit(solution)/shard_map/place/pallas_call | solution.py:655

commit v7 on v6

--- a/solution.py
+++ b/solution.py
@@ -9,7 +9,7 @@
 
 BLOCK = 64
 GROUP = 4
-UNROLL = 16
+UNROLL = 32
 RING = 4
 LANES = 128
 MESH = pl.DeviceIdType.MESH
@@ -168,11 +168,11 @@
     cblk, cdev = col_place()
     wire = Wire(send_sem, recv_sem)
     peers = [(p, d) for p in (0, 1) for d in range(RING) if (p, d) != (0, 0)]
-    met = greet([rdev(0, 0, 1)] + [rdev(p, d) for p, d in peers] + [cdev(p, d) for p, d in peers])
     loads = [pltpu.make_async_copy(a, b, load_sem.at[i]) for i, (a, b) in enumerate([
         (feat_in, feat), (values_in, vals), (weight_in, weight), (gout_in, gout)])]
     for load in loads:
         load.start()
+    met = greet([rdev(0, 0, 1)] + [rdev(p, d) for p, d in peers] + [cdev(p, d) for p, d in peers])
 
     f = lambda v: v.astype(f32)
     src, gh = (src_0, src_1), (gh_0, gh_1)
@@ -273,14 +273,14 @@
         v = [gh[h][lists[5, g * GROUP + k]] for k in range(GROUP)]
         return jnp.concatenate([x[:BLOCK // 2] for x in v] + [x[BLOCK // 2:] for x in v], axis=0)
 
-    def products(h, lhs, rhs, flags, groups, pieces):
+    def products(h, lhs, rhs, flags, groups, pieces, unroll=UNROLL):
         state = [jnp.zeros((BLOCK, LANES), f32)]
-        turns = groups // UNROLL
+        turns = groups // unroll
 
         def body(i, run):
             prods = []
-            for u in range(UNROLL):
-                g = i * UNROLL + u
+            for u in range(unroll):
+                g = i * unroll + u
                 prods.append((g, jnp.dot(lhs(g), rhs(h, g), preferred_element_type=f32)))
             for g, p in prods:
                 run = jnp.where(lists[flags, g] > 0, p, run + p)
@@ -567,7 +567,7 @@
     settle(part, 0, 3, gf, nr)
     run(sum(cs.begin(0), []))
     run(rest)
-    work = products(1, lhs_fwd, rhs_fwd, 2, gf, 3)
+    work = products(1, lhs_fwd, rhs_fwd, 2, gf, 3, 56)
     work[0]()
     each(cs.ring, 0, cs.kinds(0)[1])
     run(cs.second(0))
@@ -601,7 +601,7 @@
     each(g_pair, 0, kind_a)
     each(g_far, 0, kind_b)
     g_last(0)
-    work = products(0, lhs_bwd, rhs_bwd, 6, gb, 5)
+    work = products(0, lhs_bwd, rhs_bwd, 6, gb, 5, 64)
     work[0]()
     each(g_ring, 1, kind_a)
     each(g_pair, 1, kind_b)
@@ -619,8 +619,8 @@
     each(g_pair, 1, kind_a)
     each(g_far, 1, kind_b)
     g_last(1)
+    work = products(1, lhs_bwd, rhs_bwd, 6, gb, 3, 64)
     run(sum(rs.begin(0), []))
-    work = products(1, lhs_bwd, rhs_bwd, 6, gb, 3)
     work[0]()
     w3()
     work[1]()
@@ -645,9 +645,17 @@
 
 
 def place_kernel(*refs):
-    count = len(refs) // 2
-    for i in range(count):
-        refs[count + i][...] = refs[i][...]
+    n = len(refs) // 3
+    sems = refs[-1]
+    into = [pltpu.make_async_copy(refs[i], refs[2 * n + i], sems.at[i]) for i in range(n)]
+    onto = [pltpu.make_async_copy(refs[2 * n + i], refs[n + i], sems.at[n + i]) for i in range(n)]
+    for copy in into:
+        copy.start()
+    for i in range(n):
+        into[i].wait()
+        onto[i].start()
+    for copy in onto:
+        copy.wait()
 
 
 def place(*arrays):
@@ -655,8 +663,9 @@
     return pl.pallas_call(
         place_kernel,
         out_shape=[jax.ShapeDtypeStruct(a.shape, a.dtype) for a in arrays],
-        in_specs=[pl.BlockSpec(memory_space=VM)] * n,
-        out_specs=[pl.BlockSpec(memory_space=VM)] * n,
+        in_specs=[pl.BlockSpec(memory_space=pl.ANY)] * n,
+        out_specs=[pl.BlockSpec(memory_space=pl.ANY)] * n,
+        scratch_shapes=[pltpu.VMEM(a.shape, a.dtype) for a in arrays] + [pltpu.SemaphoreType.DMA((2 * n,))],
         compiler_params=pltpu.CompilerParams(vmem_limit_bytes=60 << 20),
         name="place",
     )(*arrays)

time: 139 us -> 135 us (0.971)
  Pallas kernels: 137 us -> 133 us
    pallas_call x1, Pallas kernels: 132 us -> 128 us  [layer(): pl.pallas_call(layer_kernel, out_shape=[jax.ShapeDtypeStruct((rows, width...]
where the time goes in v7:
time: 135 us
  Pallas kernels  133 us (99%)
  between operations  1.47 us (1%)
    pallas_call x1, Pallas kernels, layer(): pl.pallas_call(layer_kernel, out_shape=[jax.ShapeDtypeStruct((rows, width...  128 us
    pallas_call x1, Pallas kernels, make_lists(): pl.pallas_call(functools.partial(lists_kernel, tiles, nr, nc), out_shape=...  3.41 us

profile of v7, /device:TPU:0, one launch (start us, length us, event | category | flops | bytes accessed | tf_op | source)
XLA Modules:
  0.0 134.6 jit_solution(5427604199886287797)
XLA Ops:
  1.3 3.4 %lists.1 = s32[8,1280]{1,0:T(8,128)} custom-call(s32[1,1,608]{2,1,0:T(1,128)} %rows_in.1, s32[1,1,608]{2,1,0:T(1,128)} %cols_in.1, s32[1,1]{1,0:T(1,128)S(6)} %copy.10.count_ref), custom_call_target="tpu_custom_call" | custom-call | tf_op jit(solution)/shard_map/lists/pallas_call | solution.py:81
  4.7 127.7 %layer.1 = (bf16[768,256]{1,0:T(8,128)(2,1)}, bf16[768,256]{1,0:T(8,128)(2,1)}, f32[256,256]{1,0:T(8,128)}) custom-call(s32[8,1280]{1,0:T(8,128)} %lists.1, bf16[768,256]{1,0:T(8,128)(2,1)} %feat_in.1, bf16[256,256]{1,0:T(8,128)(2,1)} %weight_in.1, bf16[768,256]{1,0:T(8,128)(2,1)} %gout_in.1, bf16[608,4096]{1,0:T(8,128)(2,1)} %bitcast.1), custom_call_target="tpu_custom_call" | custom-call | tf_op jit(solution)/shard_map/layer/pallas_call | solution.py:695
  132.4 2.0 %place.1 = (bf16[768,256]{1,0:T(8,128)(2,1)}, bf16[768,256]{1,0:T(8,128)(2,1)}, f32[256,256]{1,0:T(8,128)}) custom-call(bf16[768,256]{1,0:T(8,128)(2,1)} %get-tuple-element.6.refs_0_, bf16[768,256]{1,0:T(8,128)(2,1)} %get-tuple-element.7.refs_1_, f32[256,256]{1,0:T(8,128)} %get-tuple-element.8.refs_2_), custom_call_target="tpu_custom_call" | custom-call | tf_op jit(solution)/shard_map/place/pallas_call | solution.py:663
